TPU v7x, 256 devices: a whole 4x4x8 slice. The times are simulated.
256 devices in a mesh: row: 32 (over z, x), col: 8 (over y, core).
Axes of the slice: x: 4, y: 4, z: 8, core: 2. Of those that a mesh axis runs over, the one named last changes fastest.
Arguments:
- panel_block: float32 [98304, 512], P('row', 'col'), may hold values from -1 to 1
- trailing: float32 [98304, 2048], P('row', 'col'), may hold values from -6 to 6
Outputs:
- triangle: float32 [512, 512], replicated
- coupling: float32 [512, 2048], P(None, 'col')
- updated: float32 [98304, 2048], P('row', 'col')
All inputs are finite; a program needn't handle non-finite values.
Results may differ from a plain program's by a relative error of at most 0.0003.
Values sent between devices are 32-bit elements; how exact they have to be, the bound alone decides.
No kernel may reach another device: no remote copies, remote signals or barrier semaphores. Data moves between devices by JAX's collectives and lax.ppermute only.
A program may use at most 128 MiB of HBM per device.

v0:
```python
import jax
import jax.numpy as jnp
from jax import lax
from jax.experimental import pallas as pl
from jax.experimental.pallas import tpu as pltpu
from jax.sharding import Mesh
from jax.sharding import PartitionSpec as P

highest = lax.Precision.HIGHEST
LEAF = 64
LANES = 128

def spread(v, shape):
    return jnp.broadcast_to(v, shape)

def leaf_factor(block):
    groups = LEAF // 8
    full = (8, LANES)
    sub = lax.broadcasted_iota(jnp.int32, full, 0)
    x = [block[8 * i : 8 * i + 8] for i in range(groups)]
    done = []
    for kb in range(groups):
        cols = [
            [spread(x[i][:, 8 * kb + j : 8 * kb + j + 1], full) for i in range(kb, groups)]
            for j in range(8)
        ]
        pivots = jnp.ones(full, jnp.float32)
        for j in range(8):
            pivot = spread(cols[j][0][j : j + 1], full)
            pivots = jnp.where(sub == j, pivot, pivots)
            inverse = 1.0 / pivot
            tail = [spread(cols[jj][0][j : j + 1], full) * inverse for jj in range(j + 1, 8)]
            row = spread(x[kb][j : j + 1], full) * inverse
            for i in range(kb, groups):
                mult = cols[j][i - kb]
                if i == kb:
                    mult = jnp.where(sub > j, mult, 0.0)
                for jj in range(j + 1, 8):
                    cols[jj][i - kb] = cols[jj][i - kb] - mult * tail[jj - j - 1]
                x[i] = x[i] - mult * row
        done.append(x[kb] * (1.0 / jnp.sqrt(pivots)))
    return jnp.concatenate(done, axis=0)

def factor_kernel(gram_ref, upper_ref, inverse_ref, work):
    size = gram_ref.shape[0]
    blocks = size // LEAF
    lane = lax.broadcasted_iota(jnp.int32, (LEAF, LANES), 1)
    sub = lax.broadcasted_iota(jnp.int32, (LEAF, LANES), 0)
    place = lax.broadcasted_iota(jnp.int32, (LEAF, size), 1)
    depth = lax.broadcasted_iota(jnp.int32, (LEAF, size), 0)
    work[...] = gram_ref[...]
    for b in range(blocks):
        lo, hi = LEAF * b, LEAF * b + LEAF
        tile = LANES * (b // 2)
        square = work[lo:hi, tile : tile + LANES]
        if b % 2:
            square = pltpu.roll(square, LEAF, 1)
        both = leaf_factor(
            jnp.where(lane < LEAF, square, jnp.where(lane == sub + LEAF, 1.0, 0.0))
        )
        other = pltpu.roll(both, LEAF, 1)
        inv = other[:, :LEAF]
        rows = jnp.dot(inv, work[lo:hi, :], precision=highest, preferred_element_type=jnp.float32)
        inv_wide = jnp.concatenate([both if b % 2 else other] * (size // LANES), axis=1)
        own = (place >= lo) & (place < hi)
        upper_ref[lo:hi, :] = jnp.where(place >= lo + depth, rows, 0.0)
        rows_inv = jnp.where(own, inv_wide, rows)
        inverse_ref[lo:hi, :] = jnp.where(place <= lo + depth, rows_inv, 0.0)
        if b + 1 < blocks:
            mult = rows[:, hi - hi % LANES :]
            if hi % LANES:
                mult = mult[:, LEAF:]
            step = lax.dot_general(
                mult, rows_inv, (((0,), (0,)), ((), ())),
                precision=highest, preferred_element_type=jnp.float32,
            )
            below = lax.broadcasted_iota(jnp.int32, (size - hi, size), 1)
            kept = jnp.where((below >= lo) & (below < hi), 0.0, work[hi:, :])
            work[hi:, :] = kept - step

def factor(gram):
    size = gram.shape[0]
    return pl.pallas_call(
        factor_kernel,
        out_shape=[jax.ShapeDtypeStruct((size, size), jnp.float32)] * 2,
        in_specs=[pl.BlockSpec(memory_space=pltpu.VMEM)],
        out_specs=[pl.BlockSpec(memory_space=pltpu.VMEM)] * 2,
        scratch_shapes=[pltpu.VMEM((size, size), jnp.float32)],
        compiler_params=pltpu.CompilerParams(vmem_limit_bytes=32 * 2**20),
        name="factor",
    )(gram)


def dot(left, right, left_dim, right_dim, precision):
    return lax.dot_general(
        left, right, (((left_dim,), (right_dim,)), ((), ())),
        precision=precision, preferred_element_type=jnp.float32,
    )


def sum_over_rows(pieces, peers):
    arrived = lax.all_to_all(pieces, "row", 0, 0)
    summed = jnp.sum(arrived, axis=0)
    return lax.all_to_all(jnp.broadcast_to(summed, pieces.shape), "row", 0, 0)


def on_device(panel_block, trailing, peers):
    own = panel_block.T
    width = own.shape[0]
    gathered = lax.all_gather(own, "col", axis=0, tiled=True)
    size = gathered.shape[0]
    cols = trailing.shape[1]
    projected = dot(gathered, trailing, 1, 0, lax.Precision.HIGH)
    gram = dot(own, gathered, 1, 1, lax.Precision.HIGH)
    tiles_p = projected.reshape(peers, size // peers, cols // 128, 128).transpose(0, 2, 1, 3)
    tiles_p = tiles_p.reshape(peers, -1, 128)
    tiles_g = gram.reshape(width // 8, 8, size // 128, 128).transpose(0, 2, 1, 3)
    tiles_g = tiles_g.reshape(peers, -1, 128)
    both = sum_over_rows(jnp.concatenate([tiles_p, tiles_g], axis=1), peers)
    rows_p = size // peers * (cols // 128)
    tiles_p, tiles_g = both[:, :rows_p], both[:, rows_p:]
    projected = tiles_p.reshape(peers, cols // 128, size // peers, 128).transpose(0, 2, 1, 3)
    projected = projected.reshape(size, cols)
    gram = tiles_g.reshape(width // 8, size // 128, 8, 128).transpose(0, 2, 1, 3)
    gram = gram.reshape(width, size)
    gram = lax.all_to_all(jnp.broadcast_to(gram, (size // width, width, size)), "col", 0, 0)
    upper, inverse = factor(gram.reshape(size, size))
    coupling = dot(inverse, projected, 1, 0, highest)
    weights = dot(inverse, coupling, 0, 0, highest)
    updated = trailing - dot(gathered, weights, 0, 0, lax.Precision.HIGH)
    return (upper, coupling, updated)


def solution(mesh):
    placed = (P("row", "col"), P("row", "col"))
    peers = mesh.shape["row"]
    return jax.shard_map(
        lambda panel_block, trailing: on_device(panel_block, trailing, peers),
        mesh=mesh,
        in_specs=placed,
        out_specs=(P(), P(None, "col"), P("row", "col")),
        check_vma=False,
    )
```

profile of v0, /device:TPU:1, one launch (start us, length us, event | category | flops | bytes accessed | tf_op | source)
XLA Modules:
  0.0 184.0 jit_solution(12451548073860521295)
XLA Ops:
  7.2 0.0 all-gather.2.cloned.1.call-start
  7.2 0.0 copy-start.1
  7.2 0.7 all-gather.2.cloned.1.call-update
  7.9 49.7 %all-gather.2.cloned.1.call-done = f32[512,3072]{1,0:T(8,128)} async-done(((f32[64,3072]{1,0:T(8,128)}), f32[512,3072]{1,0:T(8,128)}) %all-gather.2.cloned.1.call-update) | async-done | bytes 6291472 | tf_op jit(solution)/shard_map/all_gather | solution.py:110
  57.6 5.9 %fusion.4 = f32[512,256]{1,0:T(8,128)S(1)} fusion(f32[512,3072]{1,0:T(8,128)} %all-gather.2.cloned.1.call-done, f32[3072,256]{1,0:T(8,128)} %param.3), kind=kOutput, calls=%fused_computation.6 | convolution fusion | flops 2415919104 | bytes 9961472 | tf_op jit(solution)/shard_map/dot_general | solution.py:95
  63.5 0.3 reshape.33
  63.8 0.0 copy-done.1
  63.8 5.8 %fusion.5 = f32[64,512]{1,0:T(8,128)S(1)} fusion(f32[3072,64]{0,1:T(8,128)S(1)} %copy-done.1, f32[512,3072]{1,0:T(8,128)} %all-gather.2.cloned.1.call-done), kind=kOutput, calls=%fused_computation.7 | convolution fusion | flops 603979776 | bytes 7208960 | tf_op jit(solution)/shard_map/dot_general | solution.py:95
  69.6 28.3 %all_to_all.15 = f32[32,40,128]{2,1,0:T(8,128)S(1)} all-to-all(f32[32,40,128]{2,1,0:T(8,128)S(1)} %pad_maximum_fusion), channel_id=1, replica_groups=mesh['row'=32,'col'=8] {'row'}, dimensions={0} | all-to-all | bytes 1310720 | tf_op jit(solution)/shard_map/all_to_all | solution.py:102
  98.0 0.1 reduce_sum.9
  98.1 22.8 %all_to_all.16 = f32[32,40,128]{2,1,0:T(8,128)S(1)} all-to-all(f32[32,40,128]{2,1,0:T(8,128)S(1)} %broadcast_in_dim.6), channel_id=1, replica_groups=mesh['row'=32,'col'=8] {'row'}, dimensions={0} | all-to-all | bytes 1310720 | tf_op jit(solution)/shard_map/all_to_all | solution.py:104
  120.9 1.1 broadcast_in_dim.7
  122.0 7.2 %all-to-all-start.2 = ((f32[8,64,512]{2,1,0:T(8,128)}), f32[8,64,512]{2,1,0:T(8,128)S(1)}, u32[]{:S(2)}, u32[]{:S(2)}) async-start(f32[8,64,512]{2,1,0:T(8,128)} %broadcast_in_dim.7), calls=%async_computation.2 | async-start | bytes 2097152 | tf_op jit(solution)/shard_map/all_to_all | solution.py:126
  129.1 3.5 %copy.12 = f32[3072,256]{0,1:T(8,128)} copy(f32[3072,256]{1,0:T(8,128)} %param.3) | data formatting | bytes 6291456 | tf_op args[1]
  132.7 0.1 slice.9
  132.7 0.3 copy.11
  133.0 11.2 %all-to-all-done.2 = f32[8,64,512]{2,1,0:T(8,128)S(1)} async-done(((f32[8,64,512]{2,1,0:T(8,128)}), f32[8,64,512]{2,1,0:T(8,128)S(1)}, u32[]{:S(2)}, u32[]{:S(2)}) %all-to-all-start.2) | async-done | bytes 1048608 | tf_op jit(solution)/shard_map/all_to_all | solution.py:126
  144.2 0.0 copy-start
  144.2 22.7 %factor.1 = (f32[512,512]{1,0:T(8,128)}, f32[512,512]{1,0:T(8,128)S(1)}) custom-call(f32[512,512]{1,0:T(8,128)S(1)} %bitcast.36), custom_call_target="tpu_custom_call" | custom-call | tf_op jit(solution)/shard_map/factor/pallas_call | solution.py:83
  166.9 1.0 fusion.1
  167.9 0.0 copy-start.2
  167.9 1.8 fusion.6
  169.7 0.0 copy-done.2
  169.8 0.0 copy-done
  169.8 5.1 %fusion = f32[3072,256]{0,1:T(8,128)S(1)} fusion(f32[3072,256]{0,1:T(8,128)S(1)} %copy-done, f32[512,256]{1,0:T(8,128)S(1)} %fusion.6, f32[512,3072]{1,0:T(8,128)} %all-gather.2.cloned.1.call-done), kind=kOutput, calls=%fused_computation.1 | convolution fusion | flops 2416705536 | bytes 13107200 | tf_op jit(solution)/shard_map/dot_general | solution.py:95
  174.8 2.4 %copy.13 = f32[3072,256]{1,0:T(8,128)} copy(f32[3072,256]{0,1:T(8,128)S(1)} %fusion) | data formatting | bytes 6291456
  (4 shorter events, 0.1 us)
Async XLA Ops:
  7.2 50.4 %all-gather.2.cloned.1.call-start = ((), (), s32[]{:S(2)}) async-start(), calls=%async_computation.3 | async-start | bytes 7077888 | tf_op jit(solution)/shard_map/all_gather | solution.py:110
  7.2 56.6 %copy-start.1 = (f32[3072,64]{0,1:T(8,128)S(1)}, f32[3072,64]{0,1:T(8,128)}, u32[]{:S(2)}) copy-start(f32[3072,64]{0,1:T(8,128)} %param.2) | copy-start | bytes 2359300
  122.0 22.3 %all-to-all-start.2 = ((f32[8,64,512]{2,1,0:T(8,128)}), f32[8,64,512]{2,1,0:T(8,128)S(1)}, u32[]{:S(2)}, u32[]{:S(2)}) async-start(f32[8,64,512]{2,1,0:T(8,128)} %broadcast_in_dim.7), calls=%async_computation.2 | async-start | bytes 2097152 | tf_op jit(solution)/shard_map/all_to_all | solution.py:126
  144.2 25.5 %copy-start = (f32[3072,256]{0,1:T(8,128)S(1)}, f32[3072,256]{0,1:T(8,128)}, u32[]{:S(2)}) copy-start(f32[3072,256]{0,1:T(8,128)} %copy.12) | copy-start | bytes 9437188
  167.9 1.8 %copy-start.2 = (f32[512,256]{1,0:T(8,128)}, f32[512,256]{1,0:T(8,128)S(1)}, u32[]{:S(2)}) copy-start(f32[512,256]{1,0:T(8,128)S(1)} %fusion.1) | copy-start | bytes 1572868
Sparse Core Ops, SparseCore 0:
  9.8 47.6 all-gather.1
where the time goes:
time: 184 us
  waiting for transfers between devices  61.6 us (33%)
  blocking collectives  51.1 us (28%)
  Pallas kernels  22.7 us (12%)
  matrix products  19.5 us (11%)
  between operations  14.1 us (8%)
  local copies, waits for them, and re-layouts  7.7 us (4%)
  starting transfers between devices  7.21 us (4%)
    all_gather x1, waiting for transfers between devices, on_device(): gathered = lax.all_gather(own, 'col', axis=0, tiled=True)  49.7 us
    all_to_all x1, blocking collectives, sum_over_rows(): arrived = lax.all_to_all(pieces, 'row', 0, 0)  28.3 us
    all_to_all x1, blocking collectives, sum_over_rows(): return lax.all_to_all(jnp.broadcast_to(summed, pieces.shape), 'row', 0, 0)  22.8 us
    pallas_call x1, Pallas kernels, factor(): pl.pallas_call(factor_kernel, out_shape=[jax.ShapeDtypeStruct((size, size...  22.7 us
    dot_general x5, matrix products, dot(): lax.dot_general(left, right, (((left_dim,), (right_dim,)), ((), ())), pre...  19.5 us
    all_to_all x1, waiting for transfers between devices, on_device(): lax.all_to_all(jnp.broadcast_to(gram, (size // width, width, size)), 'col...  11.2 us
    all_to_all x1, starting transfers between devices, on_device(): lax.all_to_all(jnp.broadcast_to(gram, (size // width, width, size)), 'col...  7.17 us
    unnamed x8, local copies, waits for them, and re-layouts  5.92 us
  transfers between devices with their start and end apart: 2, of which 2 were waited for; matrix products, arithmetic and copies ran while one was open for 2% of the time, Pallas kernels for 0%

commit v1 on v0

v1 whole, which is shorter than its diff:
```python
import jax
import jax.numpy as jnp
from jax import lax
from jax.experimental import pallas as pl
from jax.experimental.pallas import tpu as pltpu
from jax.sharding import Mesh
from jax.sharding import PartitionSpec as P

LEAF = 64
LANES = 128

def spread(v, shape):
    return jnp.broadcast_to(v, shape)

def leaf_factor(block):
    groups = LEAF // 8
    full = (8, LANES)
    sub = lax.broadcasted_iota(jnp.int32, full, 0)
    x = [block[8 * i : 8 * i + 8] for i in range(groups)]
    done = []
    for kb in range(groups):
        cols = [
            [spread(x[i][:, 8 * kb + j : 8 * kb + j + 1], full) for i in range(kb, groups)]
            for j in range(8)
        ]
        pivots = jnp.ones(full, jnp.float32)
        for j in range(8):
            pivot = spread(cols[j][0][j : j + 1], full)
            pivots = jnp.where(sub == j, pivot, pivots)
            inverse = 1.0 / pivot
            tail = [spread(cols[jj][0][j : j + 1], full) * inverse for jj in range(j + 1, 8)]
            row = spread(x[kb][j : j + 1], full) * inverse
            for i in range(kb, groups):
                mult = cols[j][i - kb]
                if i == kb:
                    mult = jnp.where(sub > j, mult, 0.0)
                for jj in range(j + 1, 8):
                    cols[jj][i - kb] = cols[jj][i - kb] - mult * tail[jj - j - 1]
                x[i] = x[i] - mult * row
        done.append(x[kb] * (1.0 / jnp.sqrt(pivots)))
    return jnp.concatenate(done, axis=0)

def thirds(value):
    first = value.astype(jnp.bfloat16)
    rest = value - first.astype(jnp.float32)
    second = rest.astype(jnp.bfloat16)
    return first, second, (rest - second.astype(jnp.float32)).astype(jnp.bfloat16)


def six_left(value, axis):
    one, two, three = thirds(value)
    return jnp.concatenate([one, one, two, one, two, three], axis=axis)


def six_right(value):
    one, two, three = thirds(value)
    return jnp.concatenate([one, two, one, three, two, one], axis=0)


def factor_kernel(place_ref, mine_ref, other_ref, upper_ref, inverse_ref, work):
    size = work.shape[0]
    blocks = size // LEAF
    lane = lax.broadcasted_iota(jnp.int32, (LEAF, LANES), 1)
    sub = lax.broadcasted_iota(jnp.int32, (LEAF, LANES), 0)
    place = lax.broadcasted_iota(jnp.int32, (LEAF, size), 1)
    depth = lax.broadcasted_iota(jnp.int32, (LEAF, size), 0)
    y, core = place_ref[0], place_ref[1]
    for dy in range(4):
        owner = lax.rem(y + dy, 4)
        for ref, side in ((mine_ref, core), (other_ref, 1 - core)):
            for tile in range(ref.shape[1]):
                to = pl.multiple_of(128 * owner + 64 * side + 8 * (tile // 4), 8)
                lanes = pl.multiple_of(128 * lax.rem(owner + tile % 4, 4), 128)
                work[pl.ds(to, 8), pl.ds(lanes, 128)] = ref[dy, tile]
    for b in range(blocks):
        lo, hi = LEAF * b, LEAF * b + LEAF
        tile = LANES * (b // 2)
        square = work[lo:hi, tile : tile + LANES]
        if b % 2:
            square = pltpu.roll(square, LEAF, 1)
        both = leaf_factor(
            jnp.where(lane < LEAF, square, jnp.where(lane == sub + LEAF, 1.0, 0.0))
        )
        other = pltpu.roll(both, LEAF, 1)
        inv = other[:, :LEAF]
        rows = jnp.dot(
            six_left(inv, 1), six_right(work[lo:hi, :]), preferred_element_type=jnp.float32
        )
        inv_wide = jnp.concatenate([both if b % 2 else other] * (size // LANES), axis=1)
        own = (place >= lo) & (place < hi)
        upper_ref[lo:hi, :] = jnp.where(place >= lo + depth, rows, 0.0)
        rows_inv = jnp.where(own, inv_wide, rows)
        inverse_ref[lo:hi, :] = jnp.where(place <= lo + depth, rows_inv, 0.0)
        if b + 1 < blocks:
            mult = rows[:, hi - hi % LANES :]
            if hi % LANES:
                mult = mult[:, LEAF:]
            step = lax.dot_general(
                six_left(mult, 0), six_right(rows_inv), (((0,), (0,)), ((), ())),
                preferred_element_type=jnp.float32,
            )
            below = lax.broadcasted_iota(jnp.int32, (size - hi, size), 1)
            kept = jnp.where((below >= lo) & (below < hi), 0.0, work[hi:, :])
            work[hi:, :] = kept - step

def factor(place, mine, other):
    size = 512
    return pl.pallas_call(
        factor_kernel,
        out_shape=[jax.ShapeDtypeStruct((size, size), jnp.float32)] * 2,
        in_specs=[
            pl.BlockSpec(memory_space=pltpu.SMEM),
            pl.BlockSpec(memory_space=pltpu.VMEM),
            pl.BlockSpec(memory_space=pltpu.VMEM),
        ],
        out_specs=[pl.BlockSpec(memory_space=pltpu.VMEM)] * 2,
        scratch_shapes=[pltpu.VMEM((size, size), jnp.float32)],
        compiler_params=pltpu.CompilerParams(vmem_limit_bytes=56 * 2**20),
        cost_estimate=pl.CostEstimate(
            flops=25 * 10**9, bytes_accessed=4 * 10**6, transcendentals=0
        ),
        name="factor",
    )(place, mine, other)


STEPS = 3


def halves(value):
    high = value.astype(jnp.bfloat16)
    return high, (value - high.astype(jnp.float32)).astype(jnp.bfloat16)


def product(a, b):
    return lax.dot_general(a, b, (((1,), (0,)), ((), ())), preferred_element_type=jnp.float32)


def dot3(both, high, right):
    rows = high.shape[0]
    right_high, right_low = halves(right)
    first = product(both, right_high)
    return first[:rows] + (first[rows:] + product(high, right_low))


def dot4(both, right):
    rows, cols = both.shape[0] // 2, right.shape[1]
    four = product(both, jnp.concatenate(halves(right), axis=1))
    return four[:rows, :cols] + (four[rows:, :cols] + four[:rows, cols:] + four[rows:, cols:])


def dot6(left, right):
    rows = left.shape[0]
    left, right = thirds(left), thirds(right)
    first = product(jnp.concatenate(left, axis=0), right[0])
    second = product(jnp.concatenate(left[:2], axis=0), right[1])
    small = first[2 * rows :] + (second[rows:] + product(left[0], right[2]))
    return first[:rows] + (first[rows : 2 * rows] + second[:rows] + small)


def chunk(k, length):
    return pl.ds(pl.multiple_of(k * length, 128), length)


def fetches(k, depth, trailing_ref, trailing_buf, block_refs, block_buf, sems, starts=None):
    part = chunk(k, depth)
    copies = [pltpu.make_async_copy(trailing_ref.at[part], trailing_buf.at[part], sems.at[k, 0])]
    at = 0
    for index, ref in enumerate(block_refs):
        rows = ref.shape[0]
        to = pl.ds(at if starts is None else pl.multiple_of(starts[index], 32), rows)
        copies.append(
            pltpu.make_async_copy(ref.at[:, part], block_buf.at[to, part], sems.at[k, index + 1])
        )
        at += rows
    return copies


def start_all(*places):
    for k in range(STEPS):
        for copy in fetches(k, *places):
            copy.start()


def wait_chunk(k, *places):
    for copy in fetches(k, *places):
        copy.wait()


def accumulate(places, rows, proj_ref, gram_ref):
    depth, _, trailing_buf, _, block_buf, _ = places
    own_at = rows if block_buf.shape[0] > rows else 0
    start_all(*places)
    proj_ref[...] = jnp.zeros_like(proj_ref)
    gram_ref[...] = jnp.zeros_like(gram_ref)

    @pl.loop(0, STEPS)
    def _(k):
        wait_chunk(k, *places)
        part = chunk(k, depth)
        high, low = halves(block_buf[:rows, part])
        both = jnp.concatenate([high, low], axis=0)
        proj_ref[...] += dot3(both, high, trailing_buf[part])
        gram_ref[...] += dot4(both, block_buf[own_at : own_at + 64, part].T)


def first_kernel(trailing_ref, *refs):
    *block_refs, proj_ref, gram_ref, trailing_buf, block_buf, sems = refs
    depth = trailing_ref.shape[0] // STEPS
    places = (depth, trailing_ref, trailing_buf, block_refs, block_buf, sems)
    accumulate(places, block_buf.shape[0], proj_ref, gram_ref)


def last_kernel(core_ref, trailing_ref, *refs):
    *block_refs, proj_early, gram_early, proj_out, gram_out = refs[:-5]
    trailing_buf, block_buf, sems, proj_ref, gram_ref = refs[-5:]
    depth = trailing_ref.shape[0] // STEPS
    places = (depth, trailing_ref, trailing_buf, block_refs, block_buf, sems)
    accumulate(places, proj_ref.shape[0], proj_ref, gram_ref)

    def ordered(early, late):
        return [early[0:128], early[128:256], late, early[256:384]]

    peers, per = proj_out.shape[0], proj_out.shape[1] // 2
    proj = jnp.concatenate(ordered(proj_early[...], proj_ref[...]), axis=0)
    for side in range(2):
        part = proj[:, 128 * side : 128 * side + 128]
        proj_out[:, per * side : per * side + per, :] = part.reshape(peers, per, 128)
    for place, pair in enumerate(ordered(gram_early[...], gram_ref[...])):
        tile = pair.T
        tile = jnp.where(core_ref[0] == 1, pltpu.roll(tile, 64, 1), tile)
        for group in range(tile.shape[0] // 8):
            gram_out[4 * group + place] = tile[8 * group : 8 * group + 8]


def whole_spec(shape):
    return pl.BlockSpec(memory_space=pltpu.VMEM)


def in_place():
    return pl.BlockSpec(memory_space=pl.ANY)


def float_shape(*shape):
    return jax.ShapeDtypeStruct(shape, jnp.float32)


def buffers(trailing, rows, blocks):
    return [
        pltpu.VMEM(trailing.shape, jnp.float32),
        pltpu.VMEM((rows, trailing.shape[0]), jnp.float32),
        pltpu.SemaphoreType.DMA((STEPS, 1 + len(blocks))),
    ]


def project_first(trailing, blocks):
    rows = sum(block.shape[0] for block in blocks)
    shapes = [(rows, trailing.shape[1]), (rows, 64)]
    return pl.pallas_call(
        first_kernel,
        out_shape=[float_shape(*shape) for shape in shapes],
        in_specs=[in_place()] * (1 + len(blocks)),
        out_specs=[whole_spec(shape) for shape in shapes],
        scratch_shapes=buffers(trailing, rows, blocks),
        compiler_params=pltpu.CompilerParams(vmem_limit_bytes=56 * 2**20),
        cost_estimate=pl.CostEstimate(
            flops=15 * 10**9, bytes_accessed=6 * 10**6, transcendentals=0
        ),
        name="project_first",
    )(trailing, *blocks)


def project_last(core, trailing, own, blocks, proj_early, gram_early, peers):
    rows = sum(block.shape[0] for block in blocks)
    size = rows + proj_early.shape[0]
    per = size // peers * (trailing.shape[1] // 128)
    shapes = [(peers, per, 128), (4 * own.shape[0] // 8, 8, 128)]
    return pl.pallas_call(
        last_kernel,
        out_shape=[float_shape(*shape) for shape in shapes],
        in_specs=[
            pl.BlockSpec(memory_space=pltpu.SMEM),
            *[in_place()] * (2 + len(blocks)),
            whole_spec(proj_early.shape),
            whole_spec(gram_early.shape),
        ],
        out_specs=[whole_spec(shape) for shape in shapes],
        scratch_shapes=[
            *buffers(trailing, rows + own.shape[0], [*blocks, own]),
            pltpu.VMEM((rows, trailing.shape[1]), jnp.float32),
            pltpu.VMEM((rows, own.shape[0]), jnp.float32),
        ],
        compiler_params=pltpu.CompilerParams(vmem_limit_bytes=56 * 2**20),
        cost_estimate=pl.CostEstimate(flops=10**9, bytes_accessed=6 * 10**6, transcendentals=0),
        name="project_last",
    )(core, trailing, *blocks, own, proj_early, gram_early)


def update_kernel(place_ref, proj_ref, inverse_ref, trailing_ref, *refs):
    *block_refs, coupling_ref, updated_ref = refs[:-6]
    trailing_buf, block_buf, sems, both_ref, hold_ref, out_sems = refs[-6:]
    depth = trailing_ref.shape[0] // STEPS
    cols = coupling_ref.shape[1]
    size = inverse_ref.shape[0]
    y, core = place_ref[0], place_ref[1]

    def column(dy, other):
        return 128 * lax.rem(y + dy, 4) + 64 * lax.rem(core + other, 2)

    starts = [column(0, 0), column(0, 1)]
    for dy in range(1, 4):
        for other in range(2):
            starts += [column(dy, other), column(dy, other) + 32]
    places = (depth, trailing_ref, trailing_buf, block_refs, block_buf, sems, starts)
    start_all(*places)
    peers, per = proj_ref.shape[0], proj_ref.shape[1] // 2
    sides = [proj_ref[:, per * s : per * s + per, :].reshape(size, 128) for s in range(2)]
    proj = jnp.concatenate(sides, axis=1)
    for dy in range(4):
        for other in range(2):
            slot = 64 * (2 * dy + other)
            to = pl.multiple_of(column(dy, other), 64)
            hold_ref[pl.ds(to, 64), :] = proj[slot : slot + 64]
    inverse = inverse_ref[...]
    coupling = dot6(inverse, hold_ref[...])
    coupling_ref[...] = coupling
    both_ref[:cols], both_ref[cols:] = halves(dot6(coupling.T, inverse))

    def send(k):
        part = chunk(k, depth)
        return pltpu.make_async_copy(trailing_buf.at[part], updated_ref.at[part], out_sems.at[k])

    @pl.loop(0, STEPS)
    def _(k):
        wait_chunk(k, *places)
        part = chunk(k, depth)
        change = dot3(both_ref[...], both_ref[:cols, :], block_buf[:, part])
        trailing_buf[part] = trailing_buf[part] - change.T
        send(k).start()

    for k in range(STEPS):
        send(k).wait()


def update(place, projected, inverse, trailing, blocks):
    size, cols = inverse.shape[0], trailing.shape[1]
    return pl.pallas_call(
        update_kernel,
        out_shape=[float_shape(size, cols), float_shape(*trailing.shape)],
        in_specs=[
            pl.BlockSpec(memory_space=pltpu.SMEM),
            whole_spec(projected.shape),
            whole_spec(inverse.shape),
            *[in_place()] * (1 + len(blocks)),
        ],
        out_specs=[whole_spec((size, cols)), in_place()],
        scratch_shapes=[
            *buffers(trailing, size, blocks),
            pltpu.VMEM((2 * cols, size), jnp.bfloat16),
            pltpu.VMEM((size, cols), jnp.float32),
            pltpu.SemaphoreType.DMA((STEPS,)),
        ],
        compiler_params=pltpu.CompilerParams(vmem_limit_bytes=56 * 2**20),
        cost_estimate=pl.CostEstimate(
            flops=3 * 10**9, bytes_accessed=13 * 10**6, transcendentals=0
        ),
        name="update",
    )(place, projected, inverse, trailing, *blocks)


def shift(value, axis, length, step):
    return lax.ppermute(value, axis, [(i, (i + step) % length) for i in range(length)])


def swap(value):
    return shift(value, "core", 2, 1)


def sum_over_rows(pieces):
    summed = jnp.sum(lax.all_to_all(pieces, ("z", "x"), 0, 0), axis=0)
    return lax.all_to_all(jnp.broadcast_to(summed, pieces.shape), ("z", "x"), 0, 0)


def on_device(panel_block, trailing):
    peers = lax.axis_size(("z", "x"))
    y, core = lax.axis_index("y"), lax.axis_index("core")
    own = panel_block.T
    low, high = own[:32], own[32:]
    below = [shift(low, "y", 4, 1), shift(high, "y", 4, 1)]
    above = [shift(low, "y", 4, -1), shift(high, "y", 4, -1)]
    far = [shift(below[0], "y", 4, 1), shift(above[1], "y", 4, -1)]
    own_other = swap(own)
    below_other, above_other = ([swap(v) for v in vs] for vs in (below, above))
    near = [own, own_other, *above, *above_other, *below, *below_other]
    early, far_now = lax.optimization_barrier((project_first(trailing, near), far))
    far_other = [swap(v) for v in far_now]
    proj, gram = project_last(core[None], trailing, own, [*far, *far_other], *early, peers)
    gram = sum_over_rows(gram)
    gram, proj = lax.optimization_barrier((gram, proj))
    grams = jnp.stack([gram, *(shift(gram, "y", 4, -dy) for dy in range(1, 4))])
    proj = sum_over_rows(proj)
    upper, inverse = factor(jnp.stack([y, core]), grams, swap(grams))
    blocks = [own, own_other, *above, *above_other, *far, *far_other, *below, *below_other]
    coupling, updated = update(jnp.stack([y, core]), proj, inverse, trailing, blocks)
    return (upper, coupling, updated)


def solution(mesh):
    physical = Mesh(mesh.devices.reshape(8, 4, 4, 2), ("z", "x", "y", "core"))
    row, col = ("z", "x"), ("y", "core")
    return jax.shard_map(
        on_device,
        mesh=physical,
        in_specs=(P(row, col), P(row, col)),
        out_specs=(P(), P(None, col), P(row, col)),
        check_vma=False,
    )
```

time: 184 us -> 145 us (0.79)
  waiting for transfers between devices: 61.6 us -> 24.1 us
  starting transfers between devices: 7.21 us -> 34.5 us
  Pallas kernels: 22.7 us -> 45.2 us
  matrix products: 19.5 us -> 0 us
  blocking collectives: 51.1 us -> 33.4 us
  between operations: 14.1 us -> 0.99 us
    all_gather x1 -> x0, waiting for transfers between devices: 49.7 us -> none  [on_device(): gathered = lax.all_gather(own, 'col', axis=0, tiled=True)]
    ppermute x0 -> x17, waiting for transfers between devices: none -> 23.1 us  [shift(): lax.ppermute(value, axis, [(i, (i + step) % length) for i in range(length)])]
    pallas_call x0 -> x3, Pallas kernels: none -> 23 us  [the longest x1 10.6 us: update(): pl.pallas_call(update_kernel, out_shape=[float_shape(size, cols), float_s...]
    ppermute x0 -> x17, starting transfers between devices: none -> 21.9 us  [shift(): lax.ppermute(value, axis, [(i, (i + step) % length) for i in range(length)])]
    dot_general x5 -> x0, matrix products: 19.5 us -> none  [dot(): lax.dot_general(left, right, (((left_dim,), (right_dim,)), ((), ())), pre...]
    all_to_all x2, blocking collectives: 51.1 us -> 33.4 us  [the longest x1 20.4 us: sum_over_rows(): summed = jnp.sum(lax.all_to_all(pieces, ('z', 'x'), 0, 0), axis=0)]
    all_to_all x1 -> x2, waiting for transfers between devices: 11.2 us -> 0.96 us  [the longest x1 0.96 us: sum_over_rows(): summed = jnp.sum(lax.all_to_all(pieces, ('z', 'x'), 0, 0), axis=0)]
    all_to_all x1 -> x2, starting transfers between devices: 7.17 us -> 12.6 us  [the longest x1 8.53 us: sum_over_rows(): lax.all_to_all(jnp.broadcast_to(summed, pieces.shape), ('z', 'x'), 0, 0)]
  transfers between devices with their start and end apart: 2 -> 19, of which waited for: 2 -> 10; matrix products, arithmetic and copies ran while one was open for 2% -> 2% of each run, Pallas kernels for 0% -> 20%
where the time goes in v1:
time: 145 us
  Pallas kernels  45.2 us (31%)
  starting transfers between devices  34.5 us (24%)
  blocking collectives  33.4 us (23%)
  waiting for transfers between devices  24.1 us (17%)
  local copies, waits for them, and re-layouts  5.97 us (4%)
    ppermute x17, waiting for transfers between devices, shift(): lax.ppermute(value, axis, [(i, (i + step) % length) for i in range(length)])  23.1 us
    pallas_call x1, Pallas kernels, factor(): pl.pallas_call(factor_kernel, out_shape=[jax.ShapeDtypeStruct((size, size...  22.2 us
    ppermute x17, starting transfers between devices, shift(): lax.ppermute(value, axis, [(i, (i + step) % length) for i in range(length)])  21.9 us
    all_to_all x1, blocking collectives, sum_over_rows(): summed = jnp.sum(lax.all_to_all(pieces, ('z', 'x'), 0, 0), axis=0)  20.4 us
    all_to_all x1, blocking collectives, sum_over_rows(): lax.all_to_all(jnp.broadcast_to(summed, pieces.shape), ('z', 'x'), 0, 0)  13 us
    pallas_call x1, Pallas kernels, update(): pl.pallas_call(update_kernel, out_shape=[float_shape(size, cols), float_s...  10.6 us
    all_to_all x1, starting transfers between devices, sum_over_rows(): lax.all_to_all(jnp.broadcast_to(summed, pieces.shape), ('z', 'x'), 0, 0)  8.53 us
    pallas_call x1, Pallas kernels, project_first(): pl.pallas_call(first_kernel, out_shape=[float_shape(*shape) for shape in...  6.49 us
  transfers between devices with their start and end apart: 19, of which 10 were waited for; matrix products, arithmetic and copies ran while one was open for 2% of the time, Pallas kernels for 20%

profile of v1, /device:TPU:1, one launch (start us, length us, event | category | flops | bytes accessed | tf_op | source)
XLA Modules:
  0.0 144.9 jit_solution(12614635695556615570)
XLA Ops:
  0.6 3.3 %collective-permute-start.4 = (f32[64,3072]{1,0:T(8,128)}, f32[64,3072]{1,0:T(8,128)S(1)}, u32[]{:S(2)}, u32[]{:S(2)}) collective-permute-start(f32[64,3072]{1,0:T(8,128)} %bitcast.7), channel_id=1, source_target_pairs={{0,1},{1,0},{2,3},{3,2},{4,5},{5,4},{6,7},{7,6},{8,9},{9,8},{10,11... | collective-permute-start | bytes 2359304 | tf_op jit(solution)/shard_map/ppermute | solution.py:371
  4.0 1.2 fusion
  5.1 1.1 collective-permute-start.5
  6.2 0.5 collective-permute-start.2
  6.7 1.0 collective-permute-start
  7.7 0.5 collective-permute-start.8
  8.2 7.8 %collective-permute-done.5.refs_2_ = f32[32,3072]{1,0:T(8,128)S(1)} collective-permute-done((f32[32,3072]{1,0:T(8,128)S(1)}, f32[32,3072]{1,0:T(8,128)S(1)}, u32[]{:S(2)}, u32[]{:S(2)}) %collective-permute-start.5) | collective-permute-done | bytes 393248 | tf_op jit(solution)/shard_map/ppermute | solution.py:371
  15.9 1.2 collective-permute-start.6
  17.1 7.2 %collective-permute-done.2.refs_3_ = f32[32,3072]{1,0:T(8,128)S(1)} collective-permute-done((f32[32,3072]{1,0:T(8,128)S(1)}, f32[32,3072]{1,0:T(8,128)S(1)}, u32[]{:S(2)}, u32[]{:S(2)}) %collective-permute-start.2) | collective-permute-done | bytes 393248 | tf_op jit(solution)/shard_map/ppermute | solution.py:371
  24.4 0.8 collective-permute-start.7
  25.2 0.0 collective-permute-done.refs_6_.refs_10_
  25.2 0.1 collective-permute-start.9
  25.3 1.1 collective-permute-done.8.refs_7_.refs_11_
  26.4 1.4 collective-permute-start.10
  27.8 0.0 collective-permute-done.4.refs_1_
  27.9 2.7 %collective-permute-start.3 = (f32[32,3072]{1,0:T(8,128)S(1)}, f32[32,3072]{1,0:T(8,128)S(1)}, u32[]{:S(2)}, u32[]{:S(2)}) collective-permute-start(f32[32,3072]{1,0:T(8,128)S(1)} %collective-permute-done.2.refs_3_), channel_id=1, source_target_pairs={{0,6},{2,0},{4,2},{6,4},{1,7},{3,1},{5,3},{7,5},{8,14},{10,8},{12,... | collective-permute-start | bytes 1179656 | tf_op jit(solution)/shard_map/ppermute | solution.py:371
  30.6 0.7 copy-done.13
  31.3 0.1 copy-done.14
  31.4 0.8 copy-done.15
  32.2 6.5 %project_first.1 = (f32[384,256]{1,0:T(8,128)}, f32[384,64]{1,0:T(8,128)}) custom-call(f32[3072,256]{1,0:T(8,128)} %trailing_ref.5, f32[64,3072]{1,0:T(8,128)} %bitcast.9, f32[64,3072]{1,0:T(8,128)} %copy-done.6, f32[32,3072]{1,0:T(8,128)} %copy-done.8, f32[32,3072]{1,0:T(8,128)} %copy-done.9, f32[32,3072]{1,0:T(8,128)} %copy-done.12, ...), custom_call_target="tpu_custom_call" | custom-call | flops 15000000512 | bytes 6000000 | tf_op jit(solution)/shard_map/project_first/pallas_call | solution.py:258
  38.7 1.0 collective-permute-done.1.refs_0_.refs_6_
  39.7 0.9 collective-permute-start.11
  40.7 0.1 collective-permute-start.12
  40.8 1.2 collective-permute-done.11.refs_2_.refs_8_
  42.0 0.6 collective-permute-done.12.refs_3_.refs_9_
  42.6 0.2 copy-done.4
  42.8 0.6 copy-done.5
  43.4 6.0 %project_last.1 = (f32[32,32,128]{2,1,0:T(8,128)}, f32[32,8,128]{2,1,0:T(8,128)}) custom-call(s32[1]{0:T(128)} %bitcast.1.core_ref, f32[3072,256]{1,0:T(8,128)} %trailing_ref.5, f32[32,3072]{1,0:T(8,128)} %copy-done.2, f32[32,3072]{1,0:T(8,128)} %copy-done.3, f32[32,3072]{1,0:T(8,128)} %copy-done.4, f32[32,3072]{1,0:T(8,128)} %copy-done.5, ...), custom_call_target="tpu_custom_call" | custom-call | flops 1000000000 | bytes 6000000 | tf_op jit(solution)/shard_map/project_last/pallas_call | solution.py:277
  49.4 20.4 %all_to_all.20 = f32[32,8,128]{2,1,0:T(8,128)S(1)} all-to-all(f32[32,8,128]{2,1,0:T(8,128)} %get-tuple-element.23), channel_id=1, replica_groups=mesh['z'=8,'x'=4,'y'=4,'core'=2] {'z','x'}, dimensions={0} | all-to-all | bytes 262144 | tf_op jit(solution)/shard_map/all_to_all | solution.py:379
  69.8 13.0 %all_to_all.21 = f32[32,8,128]{2,1,0:T(8,128)S(1)} all-to-all(f32[32,8,128]{2,1,0:T(8,128)S(1)} %broadcast_in_dim.7), channel_id=1, replica_groups=mesh['z'=8,'x'=4,'y'=4,'core'=2] {'z','x'}, dimensions={0} | all-to-all | bytes 262144 | tf_op jit(solution)/shard_map/all_to_all | solution.py:380
  82.8 4.1 %all-to-all-start.2 = ((f32[32,32,128]{2,1,0:T(8,128)}), f32[32,32,128]{2,1,0:T(8,128)S(1)}, u32[]{:S(2)}, u32[]{:S(2)}) async-start(f32[32,32,128]{2,1,0:T(8,128)} %get-tuple-element.27), calls=%async_computation.2 | async-start | bytes 1048576 | tf_op jit(solution)/shard_map/all_to_all | solution.py:379
  86.9 0.1 collective-permute-start.15
  87.0 3.8 %collective-permute-start.14 = (f32[32,8,128]{2,1,0:T(8,128)S(1)}, f32[32,8,128]{2,1,0:T(8,128)S(1)}, u32[]{:S(2)}, u32[]{:S(2)}) collective-permute-start(f32[32,8,128]{2,1,0:T(8,128)S(1)} %all_to_all.21), channel_id=1, source_target_pairs={{0,4},{2,6},{4,0},{6,2},{1,5},{3,7},{5,1},{7,3},{8,12},{10,14},{12... | collective-permute-start | bytes 393224 | tf_op jit(solution)/shard_map/ppermute | solution.py:371
  90.8 1.3 collective-permute-done.15
  92.0 2.8 %collective-permute-done.14 = f32[32,8,128]{2,1,0:T(8,128)S(1)} collective-permute-done((f32[32,8,128]{2,1,0:T(8,128)S(1)}, f32[32,8,128]{2,1,0:T(8,128)S(1)}, u32[]{:S(2)}, u32[]{:S(2)}) %collective-permute-start.14) | collective-permute-done | bytes 131104 | tf_op jit(solution)/shard_map/ppermute | solution.py:371
  94.8 0.1 collective-permute-done.13
  94.9 0.1 pad_maximum_fusion.mine_ref
  94.9 0.0 copy-start
  94.9 4.4 %collective-permute-start.16 = (f32[4,32,8,128]{3,2,1,0:T(8,128)S(1)}, f32[4,32,8,128]{3,2,1,0:T(8,128)S(1)}, u32[]{:S(2)}, u32[]{:S(2)}) collective-permute-start(f32[4,32,8,128]{3,2,1,0:T(8,128)S(1)} %pad_maximum_fusion.mine_ref), channel_id=1, source_target_pairs={{0,1},{1,0},{2,3},{3,2},{4,5},{5,4},{6,7},{7,6},{8,9},{9,8},{10,11... | collective-permute-start | bytes 1572872 | tf_op jit(solution)/shard_map/ppermute | solution.py:371
  99.4 0.6 pad_add_fusion.place_ref
  100.0 1.0 all-to-all-done.2
  101.0 0.9 broadcast_in_dim.8
  101.8 8.5 %all-to-all-start.3 = ((f32[32,32,128]{2,1,0:T(8,128)}), f32[32,32,128]{2,1,0:T(8,128)S(1)}, u32[]{:S(2)}, u32[]{:S(2)}) async-start(f32[32,32,128]{2,1,0:T(8,128)} %broadcast_in_dim.8), calls=%async_computation.3 | async-start | bytes 1048576 | tf_op jit(solution)/shard_map/all_to_all | solution.py:380
  110.4 0.0 copy-start.7
  110.4 0.8 copy-done.7
  111.2 22.2 %factor.1 = (f32[512,512]{1,0:T(8,128)}, f32[512,512]{1,0:T(8,128)}) custom-call(s32[2]{0:T(128)} %pad_add_fusion.place_ref, f32[4,32,8,128]{3,2,1,0:T(8,128)} %copy-done, f32[4,32,8,128]{3,2,1,0:T(8,128)} %copy-done.7), custom_call_target="tpu_custom_call" | custom-call | flops 24999999488 | bytes 4000000 | tf_op jit(solution)/shard_map/factor/pallas_call | solution.py:108
  133.4 0.8 copy-done.1
  134.1 10.6 %update.1 = (f32[512,256]{1,0:T(8,128)}, f32[3072,256]{1,0:T(8,128)}) custom-call(s32[2]{0:T(128)} %pad_add_fusion.place_ref, f32[32,32,128]{2,1,0:T(8,128)} %copy-done.1, f32[512,512]{1,0:T(8,128)} %get-tuple-element.28.inverse_ref, f32[3072,256]{1,0:T(8,128)} %trailing_ref.5, f32[64,3072]{1,0:T(8,128)} %bitcast.11, f32[64,3072]{1,0:T(8,128)} %copy-done.6, ...), custom_call_target="tpu_custom_call" | custom-call | flops 3000000000 | bytes 13000000 | tf_op jit(solution)/shard_map/update/pallas_call | solution.py:346
  (35 shorter events, 0.2 us)
Async XLA Ops:
  0.6 27.2 %collective-permute-start.4 = (f32[64,3072]{1,0:T(8,128)}, f32[64,3072]{1,0:T(8,128)S(1)}, u32[]{:S(2)}, u32[]{:S(2)}) collective-permute-start(f32[64,3072]{1,0:T(8,128)} %bitcast.7), channel_id=1, source_target_pairs={{0,1},{1,0},{2,3},{3,2},{4,5},{5,4},{6,7},{7,6},{8,9},{9,8},{10,11... | collective-permute-start | bytes 2359304 | tf_op jit(solution)/shard_map/ppermute | solution.py:371
  5.1 10.8 %collective-permute-start.5 = (f32[32,3072]{1,0:T(8,128)S(1)}, f32[32,3072]{1,0:T(8,128)S(1)}, u32[]{:S(2)}, u32[]{:S(2)}) collective-permute-start(f32[32,3072]{1,0:T(8,128)S(1)} %get-tuple-element.32), channel_id=1, source_target_pairs={{0,6},{2,0},{4,2},{6,4},{1,7},{3,1},{5,3},{7,5},{8,14},{10,8},{12,... | collective-permute-start | bytes 1179656 | tf_op jit(solution)/shard_map/ppermute | solution.py:371
  6.2 18.2 %collective-permute-start.2 = (f32[32,3072]{1,0:T(8,128)S(1)}, f32[32,3072]{1,0:T(8,128)S(1)}, u32[]{:S(2)}, u32[]{:S(2)}) collective-permute-start(f32[32,3072]{1,0:T(8,128)S(1)} %get-tuple-element.31), channel_id=1, source_target_pairs={{0,6},{2,0},{4,2},{6,4},{1,7},{3,1},{5,3},{7,5},{8,14},{10,8},{12,... | collective-permute-start | bytes 1179656 | tf_op jit(solution)/shard_map/ppermute | solution.py:371
  6.7 18.5 %collective-permute-start = (f32[32,3072]{1,0:T(8,128)S(1)}, f32[32,3072]{1,0:T(8,128)S(1)}, u32[]{:S(2)}, u32[]{:S(2)}) collective-permute-start(f32[32,3072]{1,0:T(8,128)S(1)} %get-tuple-element.32), channel_id=1, source_target_pairs={{0,2},{2,4},{4,6},{6,0},{1,3},{3,5},{5,7},{7,1},{8,10},{10,12},{12... | collective-permute-start | bytes 1179656 | tf_op jit(solution)/shard_map/ppermute | solution.py:371
  7.7 18.7 %collective-permute-start.8 = (f32[32,3072]{1,0:T(8,128)S(1)}, f32[32,3072]{1,0:T(8,128)S(1)}, u32[]{:S(2)}, u32[]{:S(2)}) collective-permute-start(f32[32,3072]{1,0:T(8,128)S(1)} %get-tuple-element.31), channel_id=1, source_target_pairs={{0,2},{2,4},{4,6},{6,0},{1,3},{3,5},{5,7},{7,1},{8,10},{10,12},{12... | collective-permute-start | bytes 1179656 | tf_op jit(solution)/shard_map/ppermute | solution.py:371
  15.9 14.6 %copy-start.8 = (f32[32,3072]{1,0:T(8,128)}, f32[32,3072]{1,0:T(8,128)S(1)}, u32[]{:S(2)}) copy-start(f32[32,3072]{1,0:T(8,128)S(1)} %collective-permute-done.5.refs_2_) | copy-start | bytes 1179652
  15.9 11.9 %collective-permute-start.6 = (f32[32,3072]{1,0:T(8,128)S(1)}, f32[32,3072]{1,0:T(8,128)S(1)}, u32[]{:S(2)}, u32[]{:S(2)}) collective-permute-start(f32[32,3072]{1,0:T(8,128)S(1)} %collective-permute-done.5.refs_2_), channel_id=1, source_target_pairs={{0,1},{1,0},{2,3},{3,2},{4,5},{5,4},{6,7},{7,6},{8,9},{9,8},{10,11... | collective-permute-start | bytes 1179656 | tf_op jit(solution)/shard_map/ppermute | solution.py:371
  24.4 6.2 %copy-start.9 = (f32[32,3072]{1,0:T(8,128)}, f32[32,3072]{1,0:T(8,128)S(1)}, u32[]{:S(2)}) copy-start(f32[32,3072]{1,0:T(8,128)S(1)} %collective-permute-done.2.refs_3_) | copy-start | bytes 1179652
  24.4 6.2 %collective-permute-start.7 = (f32[32,3072]{1,0:T(8,128)S(1)}, f32[32,3072]{1,0:T(8,128)S(1)}, u32[]{:S(2)}, u32[]{:S(2)}) collective-permute-start(f32[32,3072]{1,0:T(8,128)S(1)} %collective-permute-done.2.refs_3_), channel_id=1, source_target_pairs={{0,1},{1,0},{2,3},{3,2},{4,5},{5,4},{6,7},{7,6},{8,9},{9,8},{10,11... | collective-permute-start | bytes 1179656 | tf_op jit(solution)/shard_map/ppermute | solution.py:371
  25.2 5.4 %copy-start.10 = (f32[32,3072]{1,0:T(8,128)}, f32[32,3072]{1,0:T(8,128)S(1)}, u32[]{:S(2)}) copy-start(f32[32,3072]{1,0:T(8,128)S(1)} %collective-permute-done.refs_6_.refs_10_) | copy-start | bytes 1179652
  25.2 5.4 %collective-permute-start.9 = (f32[32,3072]{1,0:T(8,128)S(1)}, f32[32,3072]{1,0:T(8,128)S(1)}, u32[]{:S(2)}, u32[]{:S(2)}) collective-permute-start(f32[32,3072]{1,0:T(8,128)S(1)} %collective-permute-done.refs_6_.refs_10_), channel_id=1, source_target_pairs={{0,1},{1,0},{2,3},{3,2},{4,5},{5,4},{6,7},{7,6},{8,9},{9,8},{10,11... | collective-permute-start | bytes 1179656 | tf_op jit(solution)/shard_map/ppermute | solution.py:371
  26.4 4.2 %copy-start.11 = (f32[32,3072]{1,0:T(8,128)}, f32[32,3072]{1,0:T(8,128)S(1)}, u32[]{:S(2)}) copy-start(f32[32,3072]{1,0:T(8,128)S(1)} %collective-permute-done.8.refs_7_.refs_11_) | copy-start | bytes 1179652
  26.4 4.2 %collective-permute-start.10 = (f32[32,3072]{1,0:T(8,128)S(1)}, f32[32,3072]{1,0:T(8,128)S(1)}, u32[]{:S(2)}, u32[]{:S(2)}) collective-permute-start(f32[32,3072]{1,0:T(8,128)S(1)} %collective-permute-done.8.refs_7_.refs_11_), channel_id=1, source_target_pairs={{0,1},{1,0},{2,3},{3,2},{4,5},{5,4},{6,7},{7,6},{8,9},{9,8},{10,11... | collective-permute-start | bytes 1179656 | tf_op jit(solution)/shard_map/ppermute | solution.py:371
  27.8 2.8 %copy-start.6 = (f32[64,3072]{1,0:T(8,128)}, f32[64,3072]{1,0:T(8,128)S(1)}, u32[]{:S(2)}) copy-start(f32[64,3072]{1,0:T(8,128)S(1)} %collective-permute-done.4.refs_1_) | copy-start | bytes 2359300
  27.8 11.9 %collective-permute-start.1 = (f32[32,3072]{1,0:T(8,128)S(1)}, f32[32,3072]{1,0:T(8,128)S(1)}, u32[]{:S(2)}, u32[]{:S(2)}) collective-permute-start(f32[32,3072]{1,0:T(8,128)S(1)} %collective-permute-done.refs_6_.refs_10_), channel_id=1, source_target_pairs={{0,2},{2,4},{4,6},{6,0},{1,3},{3,5},{5,7},{7,1},{8,10},{10,12},{12... | collective-permute-start | bytes 1179656 | tf_op jit(solution)/shard_map/ppermute | solution.py:371
  27.9 2.8 %copy-start.12 = (f32[32,3072]{1,0:T(8,128)}, f32[32,3072]{1,0:T(8,128)S(1)}, u32[]{:S(2)}) copy-start(f32[32,3072]{1,0:T(8,128)S(1)} %collective-permute-done.6.refs_4_) | copy-start | bytes 1179652
  27.9 11.9 %collective-permute-start.3 = (f32[32,3072]{1,0:T(8,128)S(1)}, f32[32,3072]{1,0:T(8,128)S(1)}, u32[]{:S(2)}, u32[]{:S(2)}) collective-permute-start(f32[32,3072]{1,0:T(8,128)S(1)} %collective-permute-done.2.refs_3_), channel_id=1, source_target_pairs={{0,6},{2,0},{4,2},{6,4},{1,7},{3,1},{5,3},{7,5},{8,14},{10,8},{12,... | collective-permute-start | bytes 1179656 | tf_op jit(solution)/shard_map/ppermute | solution.py:371
  30.5 0.8 copy-start.13
  30.6 0.9 copy-start.14
  31.4 0.8 copy-start.15
  39.7 2.9 %copy-start.2 = (f32[32,3072]{1,0:T(8,128)}, f32[32,3072]{1,0:T(8,128)S(1)}, u32[]{:S(2)}) copy-start(f32[32,3072]{1,0:T(8,128)S(1)} %collective-permute-done.1.refs_0_.refs_6_) | copy-start | bytes 1179652
  39.7 2.9 %copy-start.3 = (f32[32,3072]{1,0:T(8,128)}, f32[32,3072]{1,0:T(8,128)S(1)}, u32[]{:S(2)}) copy-start(f32[32,3072]{1,0:T(8,128)S(1)} %collective-permute-done.3.refs_1_.refs_7_) | copy-start | bytes 1179652
  39.7 2.3 %collective-permute-start.11 = (f32[32,3072]{1,0:T(8,128)S(1)}, f32[32,3072]{1,0:T(8,128)S(1)}, u32[]{:S(2)}, u32[]{:S(2)}) collective-permute-start(f32[32,3072]{1,0:T(8,128)S(1)} %collective-permute-done.1.refs_0_.refs_6_), channel_id=1, source_target_pairs={{0,1},{1,0},{2,3},{3,2},{4,5},{5,4},{6,7},{7,6},{8,9},{9,8},{10,11... | collective-permute-start | bytes 1179656 | tf_op jit(solution)/shard_map/ppermute | solution.py:371
  40.7 1.9 %collective-permute-start.12 = (f32[32,3072]{1,0:T(8,128)S(1)}, f32[32,3072]{1,0:T(8,128)S(1)}, u32[]{:S(2)}, u32[]{:S(2)}) collective-permute-start(f32[32,3072]{1,0:T(8,128)S(1)} %collective-permute-done.3.refs_1_.refs_7_), channel_id=1, source_target_pairs={{0,1},{1,0},{2,3},{3,2},{4,5},{5,4},{6,7},{7,6},{8,9},{9,8},{10,11... | collective-permute-start | bytes 1179656 | tf_op jit(solution)/shard_map/ppermute | solution.py:371
  42.0 0.8 copy-start.4
  42.6 0.8 copy-start.5
  82.8 18.1 %all-to-all-start.2 = ((f32[32,32,128]{2,1,0:T(8,128)}), f32[32,32,128]{2,1,0:T(8,128)S(1)}, u32[]{:S(2)}, u32[]{:S(2)}) async-start(f32[32,32,128]{2,1,0:T(8,128)} %get-tuple-element.27), calls=%async_computation.2 | async-start | bytes 1048576 | tf_op jit(solution)/shard_map/all_to_all | solution.py:379
  86.9 5.1 %collective-permute-start.15 = (f32[32,8,128]{2,1,0:T(8,128)S(1)}, f32[32,8,128]{2,1,0:T(8,128)S(1)}, u32[]{:S(2)}, u32[]{:S(2)}) collective-permute-start(f32[32,8,128]{2,1,0:T(8,128)S(1)} %all_to_all.21), channel_id=1, source_target_pairs={{0,2},{2,4},{4,6},{6,0},{1,3},{3,5},{5,7},{7,1},{8,10},{10,12},{12... | collective-permute-start | bytes 393224 | tf_op jit(solution)/shard_map/ppermute | solution.py:371
  87.0 7.8 %collective-permute-start.14 = (f32[32,8,128]{2,1,0:T(8,128)S(1)}, f32[32,8,128]{2,1,0:T(8,128)S(1)}, u32[]{:S(2)}, u32[]{:S(2)}) collective-permute-start(f32[32,8,128]{2,1,0:T(8,128)S(1)} %all_to_all.21), channel_id=1, source_target_pairs={{0,4},{2,6},{4,0},{6,2},{1,5},{3,7},{5,1},{7,3},{8,12},{10,14},{12... | collective-permute-start | bytes 393224 | tf_op jit(solution)/shard_map/ppermute | solution.py:371
  90.8 4.1 %collective-permute-start.13 = (f32[32,8,128]{2,1,0:T(8,128)S(1)}, f32[32,8,128]{2,1,0:T(8,128)S(1)}, u32[]{:S(2)}, u32[]{:S(2)}) collective-permute-start(f32[32,8,128]{2,1,0:T(8,128)S(1)} %all_to_all.21), channel_id=1, source_target_pairs={{0,6},{2,0},{4,2},{6,4},{1,7},{3,1},{5,3},{7,5},{8,14},{10,8},{12,... | collective-permute-start | bytes 393224 | tf_op jit(solution)/shard_map/ppermute | solution.py:371
  94.9 15.5 %copy-start = (f32[4,32,8,128]{3,2,1,0:T(8,128)}, f32[4,32,8,128]{3,2,1,0:T(8,128)S(1)}, u32[]{:S(2)}) copy-start(f32[4,32,8,128]{3,2,1,0:T(8,128)S(1)} %pad_maximum_fusion.mine_ref) | copy-start | bytes 1572868
  94.9 15.4 %collective-permute-start.16 = (f32[4,32,8,128]{3,2,1,0:T(8,128)S(1)}, f32[4,32,8,128]{3,2,1,0:T(8,128)S(1)}, u32[]{:S(2)}, u32[]{:S(2)}) collective-permute-start(f32[4,32,8,128]{3,2,1,0:T(8,128)S(1)} %pad_maximum_fusion.mine_ref), channel_id=1, source_target_pairs={{0,1},{1,0},{2,3},{3,2},{4,5},{5,4},{6,7},{7,6},{8,9},{9,8},{10,11... | collective-permute-start | bytes 1572872 | tf_op jit(solution)/shard_map/ppermute | solution.py:371
  101.8 31.5 %all-to-all-start.3 = ((f32[32,32,128]{2,1,0:T(8,128)}), f32[32,32,128]{2,1,0:T(8,128)S(1)}, u32[]{:S(2)}, u32[]{:S(2)}) async-start(f32[32,32,128]{2,1,0:T(8,128)} %broadcast_in_dim.8), calls=%async_computation.3 | async-start | bytes 1048576 | tf_op jit(solution)/shard_map/all_to_all | solution.py:380
  110.4 0.8 copy-start.7
  133.4 0.8 copy-start.1

commit v2 on v1

--- a/solution.py
+++ b/solution.py
@@ -1,3 +1,5 @@
+import functools
+
 import jax
 import jax.numpy as jnp
 from jax import lax
@@ -72,6 +74,7 @@
                 to = pl.multiple_of(128 * owner + 64 * side + 8 * (tile // 4), 8)
                 lanes = pl.multiple_of(128 * lax.rem(owner + tile % 4, 4), 128)
                 work[pl.ds(to, 8), pl.ds(lanes, 128)] = ref[dy, tile]
+    late = None
     for b in range(blocks):
         lo, hi = LEAF * b, LEAF * b + LEAF
         tile = LANES * (b // 2)
@@ -91,17 +94,29 @@
         upper_ref[lo:hi, :] = jnp.where(place >= lo + depth, rows, 0.0)
         rows_inv = jnp.where(own, inv_wide, rows)
         inverse_ref[lo:hi, :] = jnp.where(place <= lo + depth, rows_inv, 0.0)
+        if late is not None:
+            late()
+            late = None
         if b + 1 < blocks:
             mult = rows[:, hi - hi % LANES :]
             if hi % LANES:
                 mult = mult[:, LEAF:]
-            step = lax.dot_general(
-                six_left(mult, 0), six_right(rows_inv), (((0,), (0,)), ((), ())),
-                preferred_element_type=jnp.float32,
-            )
-            below = lax.broadcasted_iota(jnp.int32, (size - hi, size), 1)
-            kept = jnp.where((below >= lo) & (below < hi), 0.0, work[hi:, :])
-            work[hi:, :] = kept - step
+            left, right = six_left(mult, 0), six_right(rows_inv)
+            cut = min(hi + LEAF, size)
+
+            def subtract(start, stop, lo=lo, hi=hi, left=left, right=right):
+                step = lax.dot_general(
+                    left[:, start - hi : stop - hi], right, (((0,), (0,)), ((), ())),
+                    preferred_element_type=jnp.float32,
+                )
+                lanes = lax.broadcasted_iota(jnp.int32, (stop - start, size), 1)
+                kept = jnp.where((lanes >= lo) & (lanes < hi), 0.0, work[start:stop, :])
+                work[start:stop, :] = kept - step
+
+            subtract(hi, cut)
+            if cut < size:
+                late = functools.partial(subtract, cut, size)
+
 
 def factor(place, mine, other):
     size = 512
@@ -385,10 +400,12 @@
     y, core = lax.axis_index("y"), lax.axis_index("core")
     own = panel_block.T
     low, high = own[:32], own[32:]
-    below = [shift(low, "y", 4, 1), shift(high, "y", 4, 1)]
-    above = [shift(low, "y", 4, -1), shift(high, "y", 4, -1)]
-    far = [shift(below[0], "y", 4, 1), shift(above[1], "y", 4, -1)]
     own_other = swap(own)
+    below_low, above_high = shift(low, "y", 4, 1), shift(high, "y", 4, -1)
+    far = [shift(below_low, "y", 4, 1), shift(above_high, "y", 4, -1)]
+    low, high, own_other = lax.optimization_barrier((low, high, own_other))
+    below = [below_low, shift(high, "y", 4, 1)]
+    above = [shift(low, "y", 4, -1), above_high]
     below_other, above_other = ([swap(v) for v in vs] for vs in (below, above))
     near = [own, own_other, *above, *above_other, *below, *below_other]
     early, far_now = lax.optimization_barrier((project_first(trailing, near), far))

time: 145 us -> 142 us (0.979)
  waiting for transfers between devices: 24.1 us -> 19.8 us
  starting transfers between devices: 34.5 us -> 37.4 us
  blocking collectives: 33.4 us -> 31.8 us
    ppermute x17, waiting for transfers between devices: 23.1 us -> 19 us  [shift(): lax.ppermute(value, axis, [(i, (i + step) % length) for i in range(length)])]
    ppermute x17, starting transfers between devices: 21.9 us -> 24.7 us  [shift(): lax.ppermute(value, axis, [(i, (i + step) % length) for i in range(length)])]
    all_to_all x1, blocking collectives: 20.4 us -> 18.8 us  [sum_over_rows(): summed = jnp.sum(lax.all_to_all(pieces, ('z', 'x'), 0, 0), axis=0)]
  transfers between devices with their start and end apart: 19 -> 19, of which waited for: 10 -> 9; matrix products, arithmetic and copies ran while one was open for 2% -> 2% of each run, Pallas kernels for 20% -> 20%
where the time goes in v2:
time: 142 us
  Pallas kernels  44.8 us (32%)
  starting transfers between devices  37.4 us (26%)
  blocking collectives  31.8 us (22%)
  waiting for transfers between devices  19.8 us (14%)
  local copies, waits for them, and re-layouts  5.98 us (4%)
    ppermute x17, starting transfers between devices, shift(): lax.ppermute(value, axis, [(i, (i + step) % length) for i in range(length)])  24.7 us
    pallas_call x1, Pallas kernels, factor(): pl.pallas_call(factor_kernel, out_shape=[jax.ShapeDtypeStruct((size, size...  21.8 us
    ppermute x17, waiting for transfers between devices, shift(): lax.ppermute(value, axis, [(i, (i + step) % length) for i in range(length)])  19 us
    all_to_all x1, blocking collectives, sum_over_rows(): summed = jnp.sum(lax.all_to_all(pieces, ('z', 'x'), 0, 0), axis=0)  18.8 us
    all_to_all x1, blocking collectives, sum_over_rows(): lax.all_to_all(jnp.broadcast_to(summed, pieces.shape), ('z', 'x'), 0, 0)  13 us
    pallas_call x1, Pallas kernels, update(): pl.pallas_call(update_kernel, out_shape=[float_shape(size, cols), float_s...  10.6 us
    all_to_all x1, starting transfers between devices, sum_over_rows(): lax.all_to_all(jnp.broadcast_to(summed, pieces.shape), ('z', 'x'), 0, 0)  8.63 us
    pallas_call x1, Pallas kernels, project_first(): pl.pallas_call(first_kernel, out_shape=[float_shape(*shape) for shape in...  6.49 us
  transfers between devices with their start and end apart: 19, of which 9 were waited for; matrix products, arithmetic and copies ran while one was open for 2% of the time, Pallas kernels for 20%

profile of v2, /device:TPU:1, one launch (start us, length us, event | category | flops | bytes accessed | tf_op | source)
XLA Modules:
  0.0 141.6 jit_solution(3544753460460454086)
XLA Ops:
  0.6 3.3 %collective-permute-start.4 = (f32[64,3072]{1,0:T(8,128)}, f32[64,3072]{1,0:T(8,128)S(1)}, u32[]{:S(2)}, u32[]{:S(2)}) collective-permute-start(f32[64,3072]{1,0:T(8,128)} %bitcast.7), channel_id=1, source_target_pairs={{0,1},{1,0},{2,3},{3,2},{4,5},{5,4},{6,7},{7,6},{8,9},{9,8},{10,11... | collective-permute-start | bytes 2359304 | tf_op jit(solution)/shard_map/ppermute | solution.py:386
  4.0 1.2 fusion
  5.1 0.1 collective-permute-start
  5.2 2.7 %collective-permute-start.2 = (f32[32,3072]{1,0:T(8,128)S(1)}, f32[32,3072]{1,0:T(8,128)S(1)}, u32[]{:S(2)}, u32[]{:S(2)}) collective-permute-start(f32[32,3072]{1,0:T(8,128)S(1)} %get-tuple-element.22), channel_id=1, source_target_pairs={{0,6},{2,0},{4,2},{6,4},{1,7},{3,1},{5,3},{7,5},{8,14},{10,8},{12,... | collective-permute-start | bytes 1179656 | tf_op jit(solution)/shard_map/ppermute | solution.py:386
  7.9 0.0 collective-permute-done.4.refs_1_
  7.9 0.1 collective-permute-start.5
  8.0 1.4 collective-permute-start.8
  9.4 6.7 %collective-permute-done.2.refs_3_ = f32[32,3072]{1,0:T(8,128)S(1)} collective-permute-done((f32[32,3072]{1,0:T(8,128)S(1)}, f32[32,3072]{1,0:T(8,128)S(1)}, u32[]{:S(2)}, u32[]{:S(2)}) %collective-permute-start.2) | collective-permute-done | bytes 393248 | tf_op jit(solution)/shard_map/ppermute | solution.py:386
  16.1 1.8 %collective-permute-start.7 = (f32[32,3072]{1,0:T(8,128)S(1)}, f32[32,3072]{1,0:T(8,128)S(1)}, u32[]{:S(2)}, u32[]{:S(2)}) collective-permute-start(f32[32,3072]{1,0:T(8,128)S(1)} %collective-permute-done.2.refs_3_), channel_id=1, source_target_pairs={{0,1},{1,0},{2,3},{3,2},{4,5},{5,4},{6,7},{7,6},{8,9},{9,8},{10,11... | collective-permute-start | bytes 1179656 | tf_op jit(solution)/shard_map/ppermute | solution.py:386
  17.9 0.0 collective-permute-done.refs_6_.refs_10_
  17.9 0.4 collective-permute-start.9
  18.4 6.2 %collective-permute-done.5.refs_2_ = f32[32,3072]{1,0:T(8,128)S(1)} collective-permute-done((f32[32,3072]{1,0:T(8,128)S(1)}, f32[32,3072]{1,0:T(8,128)S(1)}, u32[]{:S(2)}, u32[]{:S(2)}) %collective-permute-start.5) | collective-permute-done | bytes 393248 | tf_op jit(solution)/shard_map/ppermute | solution.py:386
  24.5 1.1 collective-permute-start.6
  25.6 0.7 collective-permute-start.10
  26.4 2.9 %collective-permute-start.3 = (f32[32,3072]{1,0:T(8,128)S(1)}, f32[32,3072]{1,0:T(8,128)S(1)}, u32[]{:S(2)}, u32[]{:S(2)}) collective-permute-start(f32[32,3072]{1,0:T(8,128)S(1)} %collective-permute-done.2.refs_3_), channel_id=1, source_target_pairs={{0,6},{2,0},{4,2},{6,4},{1,7},{3,1},{5,3},{7,5},{8,14},{10,8},{12,... | collective-permute-start | bytes 1179656 | tf_op jit(solution)/shard_map/ppermute | solution.py:386
  29.3 0.7 copy-done.13
  30.0 0.1 copy-done.14
  30.2 0.8 copy-done.15
  30.9 6.5 %project_first.1 = (f32[384,256]{1,0:T(8,128)}, f32[384,64]{1,0:T(8,128)}) custom-call(f32[3072,256]{1,0:T(8,128)} %trailing_ref.5, f32[64,3072]{1,0:T(8,128)} %bitcast.9, f32[64,3072]{1,0:T(8,128)} %copy-done.6, f32[32,3072]{1,0:T(8,128)} %copy-done.10, f32[32,3072]{1,0:T(8,128)} %copy-done.9, f32[32,3072]{1,0:T(8,128)} %copy-done.14, ...), custom_call_target="tpu_custom_call" | custom-call | flops 15000000512 | bytes 6000000 | tf_op jit(solution)/shard_map/project_first/pallas_call | solution.py:273
  37.4 0.9 collective-permute-done.1.refs_0_.refs_6_
  38.3 1.0 collective-permute-start.11
  39.3 0.1 collective-permute-start.12
  39.4 1.2 collective-permute-done.11.refs_2_.refs_8_
  40.7 0.6 collective-permute-done.12.refs_3_.refs_9_
  41.2 0.2 copy-done.4
  41.4 0.6 copy-done.5
  42.0 6.0 %project_last.1 = (f32[32,32,128]{2,1,0:T(8,128)}, f32[32,8,128]{2,1,0:T(8,128)}) custom-call(s32[1]{0:T(128)} %bitcast.1.core_ref, f32[3072,256]{1,0:T(8,128)} %trailing_ref.5, f32[32,3072]{1,0:T(8,128)} %copy-done.2, f32[32,3072]{1,0:T(8,128)} %copy-done.3, f32[32,3072]{1,0:T(8,128)} %copy-done.4, f32[32,3072]{1,0:T(8,128)} %copy-done.5, ...), custom_call_target="tpu_custom_call" | custom-call | flops 1000000000 | bytes 6000000 | tf_op jit(solution)/shard_map/project_last/pallas_call | solution.py:292
  48.0 18.8 %all_to_all.20 = f32[32,8,128]{2,1,0:T(8,128)S(1)} all-to-all(f32[32,8,128]{2,1,0:T(8,128)} %get-tuple-element.29), channel_id=1, replica_groups=mesh['z'=8,'x'=4,'y'=4,'core'=2] {'z','x'}, dimensions={0} | all-to-all | bytes 262144 | tf_op jit(solution)/shard_map/all_to_all | solution.py:394
  66.9 13.0 %all_to_all.21 = f32[32,8,128]{2,1,0:T(8,128)S(1)} all-to-all(f32[32,8,128]{2,1,0:T(8,128)S(1)} %broadcast_in_dim.7), channel_id=1, replica_groups=mesh['z'=8,'x'=4,'y'=4,'core'=2] {'z','x'}, dimensions={0} | all-to-all | bytes 262144 | tf_op jit(solution)/shard_map/all_to_all | solution.py:395
  79.9 4.1 %all-to-all-start.2 = ((f32[32,32,128]{2,1,0:T(8,128)}), f32[32,32,128]{2,1,0:T(8,128)S(1)}, u32[]{:S(2)}, u32[]{:S(2)}) async-start(f32[32,32,128]{2,1,0:T(8,128)} %get-tuple-element.33), calls=%async_computation.2 | async-start | bytes 1048576 | tf_op jit(solution)/shard_map/all_to_all | solution.py:394
  83.9 1.0 collective-permute-start.15
  85.0 2.9 %collective-permute-start.14 = (f32[32,8,128]{2,1,0:T(8,128)S(1)}, f32[32,8,128]{2,1,0:T(8,128)S(1)}, u32[]{:S(2)}, u32[]{:S(2)}) collective-permute-start(f32[32,8,128]{2,1,0:T(8,128)S(1)} %all_to_all.21), channel_id=1, source_target_pairs={{0,4},{2,6},{4,0},{6,2},{1,5},{3,7},{5,1},{7,3},{8,12},{10,14},{12... | collective-permute-start | bytes 393224 | tf_op jit(solution)/shard_map/ppermute | solution.py:386
  87.9 0.8 collective-permute-start.13
  88.7 0.4 collective-permute-done.15
  89.1 2.9 %collective-permute-done.14 = f32[32,8,128]{2,1,0:T(8,128)S(1)} collective-permute-done((f32[32,8,128]{2,1,0:T(8,128)S(1)}, f32[32,8,128]{2,1,0:T(8,128)S(1)}, u32[]{:S(2)}, u32[]{:S(2)}) %collective-permute-start.14) | collective-permute-done | bytes 131104 | tf_op jit(solution)/shard_map/ppermute | solution.py:386
  91.9 0.1 collective-permute-done.13
  92.0 0.1 pad_maximum_fusion.mine_ref
  92.1 0.0 copy-start
  92.1 4.4 %collective-permute-start.16 = (f32[4,32,8,128]{3,2,1,0:T(8,128)S(1)}, f32[4,32,8,128]{3,2,1,0:T(8,128)S(1)}, u32[]{:S(2)}, u32[]{:S(2)}) collective-permute-start(f32[4,32,8,128]{3,2,1,0:T(8,128)S(1)} %pad_maximum_fusion.mine_ref), channel_id=1, source_target_pairs={{0,1},{1,0},{2,3},{3,2},{4,5},{5,4},{6,7},{7,6},{8,9},{9,8},{10,11... | collective-permute-start | bytes 1572872 | tf_op jit(solution)/shard_map/ppermute | solution.py:386
  96.5 0.6 pad_add_fusion.place_ref
  97.1 0.9 all-to-all-done.2
  98.0 0.9 broadcast_in_dim.8
  98.8 8.6 %all-to-all-start.3 = ((f32[32,32,128]{2,1,0:T(8,128)}), f32[32,32,128]{2,1,0:T(8,128)S(1)}, u32[]{:S(2)}, u32[]{:S(2)}) async-start(f32[32,32,128]{2,1,0:T(8,128)} %broadcast_in_dim.8), calls=%async_computation.3 | async-start | bytes 1048576 | tf_op jit(solution)/shard_map/all_to_all | solution.py:395
  107.5 0.0 copy-start.7
  107.5 0.8 copy-done.7
  108.3 21.8 %factor.1 = (f32[512,512]{1,0:T(8,128)}, f32[512,512]{1,0:T(8,128)}) custom-call(s32[2]{0:T(128)} %pad_add_fusion.place_ref, f32[4,32,8,128]{3,2,1,0:T(8,128)} %copy-done, f32[4,32,8,128]{3,2,1,0:T(8,128)} %copy-done.7), custom_call_target="tpu_custom_call" | custom-call | flops 24999999488 | bytes 4000000 | tf_op jit(solution)/shard_map/factor/pallas_call | solution.py:123
  130.1 0.8 copy-done.1
  130.9 10.6 %update.1 = (f32[512,256]{1,0:T(8,128)}, f32[3072,256]{1,0:T(8,128)}) custom-call(s32[2]{0:T(128)} %pad_add_fusion.place_ref, f32[32,32,128]{2,1,0:T(8,128)} %copy-done.1, f32[512,512]{1,0:T(8,128)} %get-tuple-element.34.inverse_ref, f32[3072,256]{1,0:T(8,128)} %trailing_ref.5, f32[64,3072]{1,0:T(8,128)} %bitcast.11, f32[64,3072]{1,0:T(8,128)} %copy-done.6, ...), custom_call_target="tpu_custom_call" | custom-call | flops 3000000000 | bytes 13000000 | tf_op jit(solution)/shard_map/update/pallas_call | solution.py:361
  (35 shorter events, 0.2 us)
Async XLA Ops:
  0.6 7.3 %collective-permute-start.4 = (f32[64,3072]{1,0:T(8,128)}, f32[64,3072]{1,0:T(8,128)S(1)}, u32[]{:S(2)}, u32[]{:S(2)}) collective-permute-start(f32[64,3072]{1,0:T(8,128)} %bitcast.7), channel_id=1, source_target_pairs={{0,1},{1,0},{2,3},{3,2},{4,5},{5,4},{6,7},{7,6},{8,9},{9,8},{10,11... | collective-permute-start | bytes 2359304 | tf_op jit(solution)/shard_map/ppermute | solution.py:386
  5.1 12.8 %collective-permute-start = (f32[32,3072]{1,0:T(8,128)S(1)}, f32[32,3072]{1,0:T(8,128)S(1)}, u32[]{:S(2)}, u32[]{:S(2)}) collective-permute-start(f32[32,3072]{1,0:T(8,128)S(1)} %get-tuple-element.21), channel_id=1, source_target_pairs={{0,2},{2,4},{4,6},{6,0},{1,3},{3,5},{5,7},{7,1},{8,10},{10,12},{12... | collective-permute-start | bytes 1179656 | tf_op jit(solution)/shard_map/ppermute | solution.py:386
  5.2 10.9 %collective-permute-start.2 = (f32[32,3072]{1,0:T(8,128)S(1)}, f32[32,3072]{1,0:T(8,128)S(1)}, u32[]{:S(2)}, u32[]{:S(2)}) collective-permute-start(f32[32,3072]{1,0:T(8,128)S(1)} %get-tuple-element.22), channel_id=1, source_target_pairs={{0,6},{2,0},{4,2},{6,4},{1,7},{3,1},{5,3},{7,5},{8,14},{10,8},{12,... | collective-permute-start | bytes 1179656 | tf_op jit(solution)/shard_map/ppermute | solution.py:386
  7.9 21.4 %copy-start.6 = (f32[64,3072]{1,0:T(8,128)}, f32[64,3072]{1,0:T(8,128)S(1)}, u32[]{:S(2)}) copy-start(f32[64,3072]{1,0:T(8,128)S(1)} %collective-permute-done.4.refs_1_) | copy-start | bytes 2359300
  7.9 16.6 %collective-permute-start.5 = (f32[32,3072]{1,0:T(8,128)S(1)}, f32[32,3072]{1,0:T(8,128)S(1)}, u32[]{:S(2)}, u32[]{:S(2)}) collective-permute-start(f32[32,3072]{1,0:T(8,128)S(1)} %get-tuple-element.21), channel_id=1, source_target_pairs={{0,6},{2,0},{4,2},{6,4},{1,7},{3,1},{5,3},{7,5},{8,14},{10,8},{12,... | collective-permute-start | bytes 1179656 | tf_op jit(solution)/shard_map/ppermute | solution.py:386
  8.0 17.7 %collective-permute-start.8 = (f32[32,3072]{1,0:T(8,128)S(1)}, f32[32,3072]{1,0:T(8,128)S(1)}, u32[]{:S(2)}, u32[]{:S(2)}) collective-permute-start(f32[32,3072]{1,0:T(8,128)S(1)} %get-tuple-element.22), channel_id=1, source_target_pairs={{0,2},{2,4},{4,6},{6,0},{1,3},{3,5},{5,7},{7,1},{8,10},{10,12},{12... | collective-permute-start | bytes 1179656 | tf_op jit(solution)/shard_map/ppermute | solution.py:386
  16.1 13.2 %copy-start.9 = (f32[32,3072]{1,0:T(8,128)}, f32[32,3072]{1,0:T(8,128)S(1)}, u32[]{:S(2)}) copy-start(f32[32,3072]{1,0:T(8,128)S(1)} %collective-permute-done.2.refs_3_) | copy-start | bytes 1179652
  16.1 10.3 %collective-permute-start.7 = (f32[32,3072]{1,0:T(8,128)S(1)}, f32[32,3072]{1,0:T(8,128)S(1)}, u32[]{:S(2)}, u32[]{:S(2)}) collective-permute-start(f32[32,3072]{1,0:T(8,128)S(1)} %collective-permute-done.2.refs_3_), channel_id=1, source_target_pairs={{0,1},{1,0},{2,3},{3,2},{4,5},{5,4},{6,7},{7,6},{8,9},{9,8},{10,11... | collective-permute-start | bytes 1179656 | tf_op jit(solution)/shard_map/ppermute | solution.py:386
  17.9 11.4 %copy-start.8 = (f32[32,3072]{1,0:T(8,128)}, f32[32,3072]{1,0:T(8,128)S(1)}, u32[]{:S(2)}) copy-start(f32[32,3072]{1,0:T(8,128)S(1)} %collective-permute-done.refs_6_.refs_10_) | copy-start | bytes 1179652
  17.9 11.3 %collective-permute-start.9 = (f32[32,3072]{1,0:T(8,128)S(1)}, f32[32,3072]{1,0:T(8,128)S(1)}, u32[]{:S(2)}, u32[]{:S(2)}) collective-permute-start(f32[32,3072]{1,0:T(8,128)S(1)} %collective-permute-done.refs_6_.refs_10_), channel_id=1, source_target_pairs={{0,1},{1,0},{2,3},{3,2},{4,5},{5,4},{6,7},{7,6},{8,9},{9,8},{10,11... | collective-permute-start | bytes 1179656 | tf_op jit(solution)/shard_map/ppermute | solution.py:386
  24.5 4.8 %copy-start.10 = (f32[32,3072]{1,0:T(8,128)}, f32[32,3072]{1,0:T(8,128)S(1)}, u32[]{:S(2)}) copy-start(f32[32,3072]{1,0:T(8,128)S(1)} %collective-permute-done.5.refs_2_) | copy-start | bytes 1179652
  24.5 4.7 %collective-permute-start.6 = (f32[32,3072]{1,0:T(8,128)S(1)}, f32[32,3072]{1,0:T(8,128)S(1)}, u32[]{:S(2)}, u32[]{:S(2)}) collective-permute-start(f32[32,3072]{1,0:T(8,128)S(1)} %collective-permute-done.5.refs_2_), channel_id=1, source_target_pairs={{0,1},{1,0},{2,3},{3,2},{4,5},{5,4},{6,7},{7,6},{8,9},{9,8},{10,11... | collective-permute-start | bytes 1179656 | tf_op jit(solution)/shard_map/ppermute | solution.py:386
  25.6 3.7 %copy-start.11 = (f32[32,3072]{1,0:T(8,128)}, f32[32,3072]{1,0:T(8,128)S(1)}, u32[]{:S(2)}) copy-start(f32[32,3072]{1,0:T(8,128)S(1)} %collective-permute-done.8.refs_7_.refs_11_) | copy-start | bytes 1179652
  25.6 3.6 %collective-permute-start.10 = (f32[32,3072]{1,0:T(8,128)S(1)}, f32[32,3072]{1,0:T(8,128)S(1)}, u32[]{:S(2)}, u32[]{:S(2)}) collective-permute-start(f32[32,3072]{1,0:T(8,128)S(1)} %collective-permute-done.8.refs_7_.refs_11_), channel_id=1, source_target_pairs={{0,1},{1,0},{2,3},{3,2},{4,5},{5,4},{6,7},{7,6},{8,9},{9,8},{10,11... | collective-permute-start | bytes 1179656 | tf_op jit(solution)/shard_map/ppermute | solution.py:386
  26.4 11.9 %collective-permute-start.1 = (f32[32,3072]{1,0:T(8,128)S(1)}, f32[32,3072]{1,0:T(8,128)S(1)}, u32[]{:S(2)}, u32[]{:S(2)}) collective-permute-start(f32[32,3072]{1,0:T(8,128)S(1)} %collective-permute-done.refs_6_.refs_10_), channel_id=1, source_target_pairs={{0,2},{2,4},{4,6},{6,0},{1,3},{3,5},{5,7},{7,1},{8,10},{10,12},{12... | collective-permute-start | bytes 1179656 | tf_op jit(solution)/shard_map/ppermute | solution.py:386
  26.4 3.0 %copy-start.12 = (f32[32,3072]{1,0:T(8,128)}, f32[32,3072]{1,0:T(8,128)S(1)}, u32[]{:S(2)}) copy-start(f32[32,3072]{1,0:T(8,128)S(1)} %collective-permute-done.7.refs_5_) | copy-start | bytes 1179652
  26.4 11.9 %collective-permute-start.3 = (f32[32,3072]{1,0:T(8,128)S(1)}, f32[32,3072]{1,0:T(8,128)S(1)}, u32[]{:S(2)}, u32[]{:S(2)}) collective-permute-start(f32[32,3072]{1,0:T(8,128)S(1)} %collective-permute-done.2.refs_3_), channel_id=1, source_target_pairs={{0,6},{2,0},{4,2},{6,4},{1,7},{3,1},{5,3},{7,5},{8,14},{10,8},{12,... | collective-permute-start | bytes 1179656 | tf_op jit(solution)/shard_map/ppermute | solution.py:386
  29.3 0.7 copy-start.13
  29.3 0.9 copy-start.14
  30.2 0.8 copy-start.15
  38.3 2.9 %copy-start.2 = (f32[32,3072]{1,0:T(8,128)}, f32[32,3072]{1,0:T(8,128)S(1)}, u32[]{:S(2)}) copy-start(f32[32,3072]{1,0:T(8,128)S(1)} %collective-permute-done.1.refs_0_.refs_6_) | copy-start | bytes 1179652
  38.3 2.9 %copy-start.3 = (f32[32,3072]{1,0:T(8,128)}, f32[32,3072]{1,0:T(8,128)S(1)}, u32[]{:S(2)}) copy-start(f32[32,3072]{1,0:T(8,128)S(1)} %collective-permute-done.3.refs_1_.refs_7_) | copy-start | bytes 1179652
  38.3 2.4 %collective-permute-start.11 = (f32[32,3072]{1,0:T(8,128)S(1)}, f32[32,3072]{1,0:T(8,128)S(1)}, u32[]{:S(2)}, u32[]{:S(2)}) collective-permute-start(f32[32,3072]{1,0:T(8,128)S(1)} %collective-permute-done.1.refs_0_.refs_6_), channel_id=1, source_target_pairs={{0,1},{1,0},{2,3},{3,2},{4,5},{5,4},{6,7},{7,6},{8,9},{9,8},{10,11... | collective-permute-start | bytes 1179656 | tf_op jit(solution)/shard_map/ppermute | solution.py:386
  39.3 1.9 %collective-permute-start.12 = (f32[32,3072]{1,0:T(8,128)S(1)}, f32[32,3072]{1,0:T(8,128)S(1)}, u32[]{:S(2)}, u32[]{:S(2)}) collective-permute-start(f32[32,3072]{1,0:T(8,128)S(1)} %collective-permute-done.3.refs_1_.refs_7_), channel_id=1, source_target_pairs={{0,1},{1,0},{2,3},{3,2},{4,5},{5,4},{6,7},{7,6},{8,9},{9,8},{10,11... | collective-permute-start | bytes 1179656 | tf_op jit(solution)/shard_map/ppermute | solution.py:386
  40.7 0.8 copy-start.4
  41.2 0.8 copy-start.5
  79.9 18.1 %all-to-all-start.2 = ((f32[32,32,128]{2,1,0:T(8,128)}), f32[32,32,128]{2,1,0:T(8,128)S(1)}, u32[]{:S(2)}, u32[]{:S(2)}) async-start(f32[32,32,128]{2,1,0:T(8,128)} %get-tuple-element.33), calls=%async_computation.2 | async-start | bytes 1048576 | tf_op jit(solution)/shard_map/all_to_all | solution.py:394
  83.9 5.1 %collective-permute-start.15 = (f32[32,8,128]{2,1,0:T(8,128)S(1)}, f32[32,8,128]{2,1,0:T(8,128)S(1)}, u32[]{:S(2)}, u32[]{:S(2)}) collective-permute-start(f32[32,8,128]{2,1,0:T(8,128)S(1)} %all_to_all.21), channel_id=1, source_target_pairs={{0,2},{2,4},{4,6},{6,0},{1,3},{3,5},{5,7},{7,1},{8,10},{10,12},{12... | collective-permute-start | bytes 393224 | tf_op jit(solution)/shard_map/ppermute | solution.py:386
  85.0 7.0 %collective-permute-start.14 = (f32[32,8,128]{2,1,0:T(8,128)S(1)}, f32[32,8,128]{2,1,0:T(8,128)S(1)}, u32[]{:S(2)}, u32[]{:S(2)}) collective-permute-start(f32[32,8,128]{2,1,0:T(8,128)S(1)} %all_to_all.21), channel_id=1, source_target_pairs={{0,4},{2,6},{4,0},{6,2},{1,5},{3,7},{5,1},{7,3},{8,12},{10,14},{12... | collective-permute-start | bytes 393224 | tf_op jit(solution)/shard_map/ppermute | solution.py:386
  87.9 4.1 %collective-permute-start.13 = (f32[32,8,128]{2,1,0:T(8,128)S(1)}, f32[32,8,128]{2,1,0:T(8,128)S(1)}, u32[]{:S(2)}, u32[]{:S(2)}) collective-permute-start(f32[32,8,128]{2,1,0:T(8,128)S(1)} %all_to_all.21), channel_id=1, source_target_pairs={{0,6},{2,0},{4,2},{6,4},{1,7},{3,1},{5,3},{7,5},{8,14},{10,8},{12,... | collective-permute-start | bytes 393224 | tf_op jit(solution)/shard_map/ppermute | solution.py:386
  92.1 15.4 %copy-start = (f32[4,32,8,128]{3,2,1,0:T(8,128)}, f32[4,32,8,128]{3,2,1,0:T(8,128)S(1)}, u32[]{:S(2)}) copy-start(f32[4,32,8,128]{3,2,1,0:T(8,128)S(1)} %pad_maximum_fusion.mine_ref) | copy-start | bytes 1572868
  92.1 15.4 %collective-permute-start.16 = (f32[4,32,8,128]{3,2,1,0:T(8,128)S(1)}, f32[4,32,8,128]{3,2,1,0:T(8,128)S(1)}, u32[]{:S(2)}, u32[]{:S(2)}) collective-permute-start(f32[4,32,8,128]{3,2,1,0:T(8,128)S(1)} %pad_maximum_fusion.mine_ref), channel_id=1, source_target_pairs={{0,1},{1,0},{2,3},{3,2},{4,5},{5,4},{6,7},{7,6},{8,9},{9,8},{10,11... | collective-permute-start | bytes 1572872 | tf_op jit(solution)/shard_map/ppermute | solution.py:386
  98.8 31.3 %all-to-all-start.3 = ((f32[32,32,128]{2,1,0:T(8,128)}), f32[32,32,128]{2,1,0:T(8,128)S(1)}, u32[]{:S(2)}, u32[]{:S(2)}) async-start(f32[32,32,128]{2,1,0:T(8,128)} %broadcast_in_dim.8), calls=%async_computation.3 | async-start | bytes 1048576 | tf_op jit(solution)/shard_map/all_to_all | solution.py:395
  107.5 0.8 copy-start.7
  130.1 0.8 copy-start.1

commit v3 on v2

--- a/solution.py
+++ b/solution.py
@@ -138,7 +138,7 @@
     )(place, mine, other)
 
 
-STEPS = 3
+STEPS = 2
 
 
 def halves(value):

time: 142 us -> 141 us (level)
  no operation moved by 1% of the time
where the time goes in v3:
time: 141 us
  Pallas kernels  44.3 us (31%)
  starting transfers between devices  37.2 us (26%)
  blocking collectives  31.8 us (23%)
  waiting for transfers between devices  19.8 us (14%)
  local copies, waits for them, and re-layouts  5.98 us (4%)
    ppermute x17, starting transfers between devices, shift(): lax.ppermute(value, axis, [(i, (i + step) % length) for i in range(length)])  24.7 us
    pallas_call x1, Pallas kernels, factor(): pl.pallas_call(factor_kernel, out_shape=[jax.ShapeDtypeStruct((size, size...  21.8 us
    ppermute x17, waiting for transfers between devices, shift(): lax.ppermute(value, axis, [(i, (i + step) % length) for i in range(length)])  18.9 us
    all_to_all x1, blocking collectives, sum_over_rows(): summed = jnp.sum(lax.all_to_all(pieces, ('z', 'x'), 0, 0), axis=0)  18.8 us
    all_to_all x1, blocking collectives, sum_over_rows(): lax.all_to_all(jnp.broadcast_to(summed, pieces.shape), ('z', 'x'), 0, 0)  13 us
    pallas_call x1, Pallas kernels, update(): pl.pallas_call(update_kernel, out_shape=[float_shape(size, cols), float_s...  10.3 us
    all_to_all x1, starting transfers between devices, sum_over_rows(): lax.all_to_all(jnp.broadcast_to(summed, pieces.shape), ('z', 'x'), 0, 0)  8.62 us
    pallas_call x1, Pallas kernels, project_first(): pl.pallas_call(first_kernel, out_shape=[float_shape(*shape) for shape in...  6.54 us
  transfers between devices with their start and end apart: 19, of which 9 were waited for; matrix products, arithmetic and copies ran while one was open for 2% of the time, Pallas kernels for 20%

profile of v3, /device:TPU:1, one launch (start us, length us, event | category | flops | bytes accessed | tf_op | source)
XLA Modules:
  0.0 140.9 jit_solution(5750779227453238270)
XLA Ops:
  0.6 3.3 %collective-permute-start.4 = (f32[64,3072]{1,0:T(8,128)}, f32[64,3072]{1,0:T(8,128)S(1)}, u32[]{:S(2)}, u32[]{:S(2)}) collective-permute-start(f32[64,3072]{1,0:T(8,128)} %bitcast.7), channel_id=1, source_target_pairs={{0,1},{1,0},{2,3},{3,2},{4,5},{5,4},{6,7},{7,6},{8,9},{9,8},{10,11... | collective-permute-start | bytes 2359304 | tf_op jit(solution)/shard_map/ppermute | solution.py:386
  4.0 1.2 fusion
  5.1 0.1 collective-permute-start
  5.2 2.7 %collective-permute-start.2 = (f32[32,3072]{1,0:T(8,128)S(1)}, f32[32,3072]{1,0:T(8,128)S(1)}, u32[]{:S(2)}, u32[]{:S(2)}) collective-permute-start(f32[32,3072]{1,0:T(8,128)S(1)} %get-tuple-element.22), channel_id=1, source_target_pairs={{0,6},{2,0},{4,2},{6,4},{1,7},{3,1},{5,3},{7,5},{8,14},{10,8},{12,... | collective-permute-start | bytes 1179656 | tf_op jit(solution)/shard_map/ppermute | solution.py:386
  7.9 0.0 collective-permute-done.4.refs_1_
  7.9 0.1 collective-permute-start.5
  8.0 1.4 collective-permute-start.8
  9.4 6.7 %collective-permute-done.2.refs_3_ = f32[32,3072]{1,0:T(8,128)S(1)} collective-permute-done((f32[32,3072]{1,0:T(8,128)S(1)}, f32[32,3072]{1,0:T(8,128)S(1)}, u32[]{:S(2)}, u32[]{:S(2)}) %collective-permute-start.2) | collective-permute-done | bytes 393248 | tf_op jit(solution)/shard_map/ppermute | solution.py:386
  16.1 1.8 %collective-permute-start.7 = (f32[32,3072]{1,0:T(8,128)S(1)}, f32[32,3072]{1,0:T(8,128)S(1)}, u32[]{:S(2)}, u32[]{:S(2)}) collective-permute-start(f32[32,3072]{1,0:T(8,128)S(1)} %collective-permute-done.2.refs_3_), channel_id=1, source_target_pairs={{0,1},{1,0},{2,3},{3,2},{4,5},{5,4},{6,7},{7,6},{8,9},{9,8},{10,11... | collective-permute-start | bytes 1179656 | tf_op jit(solution)/shard_map/ppermute | solution.py:386
  17.9 0.0 collective-permute-done.refs_6_.refs_10_
  17.9 0.4 collective-permute-start.9
  18.4 6.2 %collective-permute-done.5.refs_2_ = f32[32,3072]{1,0:T(8,128)S(1)} collective-permute-done((f32[32,3072]{1,0:T(8,128)S(1)}, f32[32,3072]{1,0:T(8,128)S(1)}, u32[]{:S(2)}, u32[]{:S(2)}) %collective-permute-start.5) | collective-permute-done | bytes 393248 | tf_op jit(solution)/shard_map/ppermute | solution.py:386
  24.5 1.1 collective-permute-start.6
  25.6 0.7 collective-permute-start.10
  26.4 2.9 %collective-permute-start.3 = (f32[32,3072]{1,0:T(8,128)S(1)}, f32[32,3072]{1,0:T(8,128)S(1)}, u32[]{:S(2)}, u32[]{:S(2)}) collective-permute-start(f32[32,3072]{1,0:T(8,128)S(1)} %collective-permute-done.2.refs_3_), channel_id=1, source_target_pairs={{0,6},{2,0},{4,2},{6,4},{1,7},{3,1},{5,3},{7,5},{8,14},{10,8},{12,... | collective-permute-start | bytes 1179656 | tf_op jit(solution)/shard_map/ppermute | solution.py:386
  29.3 0.7 copy-done.13
  30.0 0.1 copy-done.14
  30.2 0.8 copy-done.15
  30.9 6.5 %project_first.1 = (f32[384,256]{1,0:T(8,128)}, f32[384,64]{1,0:T(8,128)}) custom-call(f32[3072,256]{1,0:T(8,128)} %trailing_ref.5, f32[64,3072]{1,0:T(8,128)} %bitcast.9, f32[64,3072]{1,0:T(8,128)} %copy-done.6, f32[32,3072]{1,0:T(8,128)} %copy-done.10, f32[32,3072]{1,0:T(8,128)} %copy-done.9, f32[32,3072]{1,0:T(8,128)} %copy-done.14, ...), custom_call_target="tpu_custom_call" | custom-call | flops 15000000512 | bytes 6000000 | tf_op jit(solution)/shard_map/project_first/pallas_call | solution.py:273
  37.5 0.8 collective-permute-done.1.refs_0_.refs_6_
  38.3 1.0 collective-permute-start.11
  39.3 0.1 collective-permute-start.12
  39.4 1.2 collective-permute-done.11.refs_2_.refs_8_
  40.7 0.6 collective-permute-done.12.refs_3_.refs_9_
  41.2 0.2 copy-done.4
  41.4 0.6 copy-done.5
  42.0 5.8 %project_last.1 = (f32[32,32,128]{2,1,0:T(8,128)}, f32[32,8,128]{2,1,0:T(8,128)}) custom-call(s32[1]{0:T(128)} %bitcast.1.core_ref, f32[3072,256]{1,0:T(8,128)} %trailing_ref.5, f32[32,3072]{1,0:T(8,128)} %copy-done.2, f32[32,3072]{1,0:T(8,128)} %copy-done.3, f32[32,3072]{1,0:T(8,128)} %copy-done.4, f32[32,3072]{1,0:T(8,128)} %copy-done.5, ...), custom_call_target="tpu_custom_call" | custom-call | flops 1000000000 | bytes 6000000 | tf_op jit(solution)/shard_map/project_last/pallas_call | solution.py:292
  47.8 18.8 %all_to_all.20 = f32[32,8,128]{2,1,0:T(8,128)S(1)} all-to-all(f32[32,8,128]{2,1,0:T(8,128)} %get-tuple-element.29), channel_id=1, replica_groups=mesh['z'=8,'x'=4,'y'=4,'core'=2] {'z','x'}, dimensions={0} | all-to-all | bytes 262144 | tf_op jit(solution)/shard_map/all_to_all | solution.py:394
  66.6 13.0 %all_to_all.21 = f32[32,8,128]{2,1,0:T(8,128)S(1)} all-to-all(f32[32,8,128]{2,1,0:T(8,128)S(1)} %broadcast_in_dim.7), channel_id=1, replica_groups=mesh['z'=8,'x'=4,'y'=4,'core'=2] {'z','x'}, dimensions={0} | all-to-all | bytes 262144 | tf_op jit(solution)/shard_map/all_to_all | solution.py:395
  79.6 3.9 %all-to-all-start.2 = ((f32[32,32,128]{2,1,0:T(8,128)}), f32[32,32,128]{2,1,0:T(8,128)S(1)}, u32[]{:S(2)}, u32[]{:S(2)}) async-start(f32[32,32,128]{2,1,0:T(8,128)} %get-tuple-element.33), calls=%async_computation.2 | async-start | bytes 1048576 | tf_op jit(solution)/shard_map/all_to_all | solution.py:394
  83.5 1.0 collective-permute-start.15
  84.5 2.9 %collective-permute-start.14 = (f32[32,8,128]{2,1,0:T(8,128)S(1)}, f32[32,8,128]{2,1,0:T(8,128)S(1)}, u32[]{:S(2)}, u32[]{:S(2)}) collective-permute-start(f32[32,8,128]{2,1,0:T(8,128)S(1)} %all_to_all.21), channel_id=1, source_target_pairs={{0,4},{2,6},{4,0},{6,2},{1,5},{3,7},{5,1},{7,3},{8,12},{10,14},{12... | collective-permute-start | bytes 393224 | tf_op jit(solution)/shard_map/ppermute | solution.py:386
  87.5 0.8 collective-permute-start.13
  88.2 0.4 collective-permute-done.15
  88.6 2.9 %collective-permute-done.14 = f32[32,8,128]{2,1,0:T(8,128)S(1)} collective-permute-done((f32[32,8,128]{2,1,0:T(8,128)S(1)}, f32[32,8,128]{2,1,0:T(8,128)S(1)}, u32[]{:S(2)}, u32[]{:S(2)}) %collective-permute-start.14) | collective-permute-done | bytes 131104 | tf_op jit(solution)/shard_map/ppermute | solution.py:386
  91.5 0.1 collective-permute-done.13
  91.6 0.1 pad_maximum_fusion.mine_ref
  91.6 0.0 copy-start
  91.6 4.4 %collective-permute-start.16 = (f32[4,32,8,128]{3,2,1,0:T(8,128)S(1)}, f32[4,32,8,128]{3,2,1,0:T(8,128)S(1)}, u32[]{:S(2)}, u32[]{:S(2)}) collective-permute-start(f32[4,32,8,128]{3,2,1,0:T(8,128)S(1)} %pad_maximum_fusion.mine_ref), channel_id=1, source_target_pairs={{0,1},{1,0},{2,3},{3,2},{4,5},{5,4},{6,7},{7,6},{8,9},{9,8},{10,11... | collective-permute-start | bytes 1572872 | tf_op jit(solution)/shard_map/ppermute | solution.py:386
  96.0 0.6 pad_add_fusion.place_ref
  96.7 0.9 all-to-all-done.2
  97.6 0.9 broadcast_in_dim.8
  98.4 8.6 %all-to-all-start.3 = ((f32[32,32,128]{2,1,0:T(8,128)}), f32[32,32,128]{2,1,0:T(8,128)S(1)}, u32[]{:S(2)}, u32[]{:S(2)}) async-start(f32[32,32,128]{2,1,0:T(8,128)} %broadcast_in_dim.8), calls=%async_computation.3 | async-start | bytes 1048576 | tf_op jit(solution)/shard_map/all_to_all | solution.py:395
  107.1 0.0 copy-start.7
  107.1 0.8 copy-done.7
  107.9 21.8 %factor.1 = (f32[512,512]{1,0:T(8,128)}, f32[512,512]{1,0:T(8,128)}) custom-call(s32[2]{0:T(128)} %pad_add_fusion.place_ref, f32[4,32,8,128]{3,2,1,0:T(8,128)} %copy-done, f32[4,32,8,128]{3,2,1,0:T(8,128)} %copy-done.7), custom_call_target="tpu_custom_call" | custom-call | flops 24999999488 | bytes 4000000 | tf_op jit(solution)/shard_map/factor/pallas_call | solution.py:123
  129.7 0.8 copy-done.1
  130.5 10.3 %update.1 = (f32[512,256]{1,0:T(8,128)}, f32[3072,256]{1,0:T(8,128)}) custom-call(s32[2]{0:T(128)} %pad_add_fusion.place_ref, f32[32,32,128]{2,1,0:T(8,128)} %copy-done.1, f32[512,512]{1,0:T(8,128)} %get-tuple-element.34.inverse_ref, f32[3072,256]{1,0:T(8,128)} %trailing_ref.5, f32[64,3072]{1,0:T(8,128)} %bitcast.11, f32[64,3072]{1,0:T(8,128)} %copy-done.6, ...), custom_call_target="tpu_custom_call" | custom-call | flops 3000000000 | bytes 13000000 | tf_op jit(solution)/shard_map/update/pallas_call | solution.py:361
  (35 shorter events, 0.2 us)
Async XLA Ops:
  0.6 7.3 %collective-permute-start.4 = (f32[64,3072]{1,0:T(8,128)}, f32[64,3072]{1,0:T(8,128)S(1)}, u32[]{:S(2)}, u32[]{:S(2)}) collective-permute-start(f32[64,3072]{1,0:T(8,128)} %bitcast.7), channel_id=1, source_target_pairs={{0,1},{1,0},{2,3},{3,2},{4,5},{5,4},{6,7},{7,6},{8,9},{9,8},{10,11... | collective-permute-start | bytes 2359304 | tf_op jit(solution)/shard_map/ppermute | solution.py:386
  5.1 12.8 %collective-permute-start = (f32[32,3072]{1,0:T(8,128)S(1)}, f32[32,3072]{1,0:T(8,128)S(1)}, u32[]{:S(2)}, u32[]{:S(2)}) collective-permute-start(f32[32,3072]{1,0:T(8,128)S(1)} %get-tuple-element.21), channel_id=1, source_target_pairs={{0,2},{2,4},{4,6},{6,0},{1,3},{3,5},{5,7},{7,1},{8,10},{10,12},{12... | collective-permute-start | bytes 1179656 | tf_op jit(solution)/shard_map/ppermute | solution.py:386
  5.2 10.9 %collective-permute-start.2 = (f32[32,3072]{1,0:T(8,128)S(1)}, f32[32,3072]{1,0:T(8,128)S(1)}, u32[]{:S(2)}, u32[]{:S(2)}) collective-permute-start(f32[32,3072]{1,0:T(8,128)S(1)} %get-tuple-element.22), channel_id=1, source_target_pairs={{0,6},{2,0},{4,2},{6,4},{1,7},{3,1},{5,3},{7,5},{8,14},{10,8},{12,... | collective-permute-start | bytes 1179656 | tf_op jit(solution)/shard_map/ppermute | solution.py:386
  7.9 21.4 %copy-start.6 = (f32[64,3072]{1,0:T(8,128)}, f32[64,3072]{1,0:T(8,128)S(1)}, u32[]{:S(2)}) copy-start(f32[64,3072]{1,0:T(8,128)S(1)} %collective-permute-done.4.refs_1_) | copy-start | bytes 2359300
  7.9 16.6 %collective-permute-start.5 = (f32[32,3072]{1,0:T(8,128)S(1)}, f32[32,3072]{1,0:T(8,128)S(1)}, u32[]{:S(2)}, u32[]{:S(2)}) collective-permute-start(f32[32,3072]{1,0:T(8,128)S(1)} %get-tuple-element.21), channel_id=1, source_target_pairs={{0,6},{2,0},{4,2},{6,4},{1,7},{3,1},{5,3},{7,5},{8,14},{10,8},{12,... | collective-permute-start | bytes 1179656 | tf_op jit(solution)/shard_map/ppermute | solution.py:386
  8.0 17.7 %collective-permute-start.8 = (f32[32,3072]{1,0:T(8,128)S(1)}, f32[32,3072]{1,0:T(8,128)S(1)}, u32[]{:S(2)}, u32[]{:S(2)}) collective-permute-start(f32[32,3072]{1,0:T(8,128)S(1)} %get-tuple-element.22), channel_id=1, source_target_pairs={{0,2},{2,4},{4,6},{6,0},{1,3},{3,5},{5,7},{7,1},{8,10},{10,12},{12... | collective-permute-start | bytes 1179656 | tf_op jit(solution)/shard_map/ppermute | solution.py:386
  16.1 13.2 %copy-start.9 = (f32[32,3072]{1,0:T(8,128)}, f32[32,3072]{1,0:T(8,128)S(1)}, u32[]{:S(2)}) copy-start(f32[32,3072]{1,0:T(8,128)S(1)} %collective-permute-done.2.refs_3_) | copy-start | bytes 1179652
  16.1 10.3 %collective-permute-start.7 = (f32[32,3072]{1,0:T(8,128)S(1)}, f32[32,3072]{1,0:T(8,128)S(1)}, u32[]{:S(2)}, u32[]{:S(2)}) collective-permute-start(f32[32,3072]{1,0:T(8,128)S(1)} %collective-permute-done.2.refs_3_), channel_id=1, source_target_pairs={{0,1},{1,0},{2,3},{3,2},{4,5},{5,4},{6,7},{7,6},{8,9},{9,8},{10,11... | collective-permute-start | bytes 1179656 | tf_op jit(solution)/shard_map/ppermute | solution.py:386
  17.9 11.4 %copy-start.8 = (f32[32,3072]{1,0:T(8,128)}, f32[32,3072]{1,0:T(8,128)S(1)}, u32[]{:S(2)}) copy-start(f32[32,3072]{1,0:T(8,128)S(1)} %collective-permute-done.refs_6_.refs_10_) | copy-start | bytes 1179652
  17.9 11.3 %collective-permute-start.9 = (f32[32,3072]{1,0:T(8,128)S(1)}, f32[32,3072]{1,0:T(8,128)S(1)}, u32[]{:S(2)}, u32[]{:S(2)}) collective-permute-start(f32[32,3072]{1,0:T(8,128)S(1)} %collective-permute-done.refs_6_.refs_10_), channel_id=1, source_target_pairs={{0,1},{1,0},{2,3},{3,2},{4,5},{5,4},{6,7},{7,6},{8,9},{9,8},{10,11... | collective-permute-start | bytes 1179656 | tf_op jit(solution)/shard_map/ppermute | solution.py:386
  24.5 4.8 %copy-start.10 = (f32[32,3072]{1,0:T(8,128)}, f32[32,3072]{1,0:T(8,128)S(1)}, u32[]{:S(2)}) copy-start(f32[32,3072]{1,0:T(8,128)S(1)} %collective-permute-done.5.refs_2_) | copy-start | bytes 1179652
  24.5 4.7 %collective-permute-start.6 = (f32[32,3072]{1,0:T(8,128)S(1)}, f32[32,3072]{1,0:T(8,128)S(1)}, u32[]{:S(2)}, u32[]{:S(2)}) collective-permute-start(f32[32,3072]{1,0:T(8,128)S(1)} %collective-permute-done.5.refs_2_), channel_id=1, source_target_pairs={{0,1},{1,0},{2,3},{3,2},{4,5},{5,4},{6,7},{7,6},{8,9},{9,8},{10,11... | collective-permute-start | bytes 1179656 | tf_op jit(solution)/shard_map/ppermute | solution.py:386
  25.6 3.7 %copy-start.11 = (f32[32,3072]{1,0:T(8,128)}, f32[32,3072]{1,0:T(8,128)S(1)}, u32[]{:S(2)}) copy-start(f32[32,3072]{1,0:T(8,128)S(1)} %collective-permute-done.8.refs_7_.refs_11_) | copy-start | bytes 1179652
  25.6 3.6 %collective-permute-start.10 = (f32[32,3072]{1,0:T(8,128)S(1)}, f32[32,3072]{1,0:T(8,128)S(1)}, u32[]{:S(2)}, u32[]{:S(2)}) collective-permute-start(f32[32,3072]{1,0:T(8,128)S(1)} %collective-permute-done.8.refs_7_.refs_11_), channel_id=1, source_target_pairs={{0,1},{1,0},{2,3},{3,2},{4,5},{5,4},{6,7},{7,6},{8,9},{9,8},{10,11... | collective-permute-start | bytes 1179656 | tf_op jit(solution)/shard_map/ppermute | solution.py:386
  26.4 11.9 %collective-permute-start.1 = (f32[32,3072]{1,0:T(8,128)S(1)}, f32[32,3072]{1,0:T(8,128)S(1)}, u32[]{:S(2)}, u32[]{:S(2)}) collective-permute-start(f32[32,3072]{1,0:T(8,128)S(1)} %collective-permute-done.refs_6_.refs_10_), channel_id=1, source_target_pairs={{0,2},{2,4},{4,6},{6,0},{1,3},{3,5},{5,7},{7,1},{8,10},{10,12},{12... | collective-permute-start | bytes 1179656 | tf_op jit(solution)/shard_map/ppermute | solution.py:386
  26.4 3.0 %copy-start.12 = (f32[32,3072]{1,0:T(8,128)}, f32[32,3072]{1,0:T(8,128)S(1)}, u32[]{:S(2)}) copy-start(f32[32,3072]{1,0:T(8,128)S(1)} %collective-permute-done.7.refs_5_) | copy-start | bytes 1179652
  26.4 11.9 %collective-permute-start.3 = (f32[32,3072]{1,0:T(8,128)S(1)}, f32[32,3072]{1,0:T(8,128)S(1)}, u32[]{:S(2)}, u32[]{:S(2)}) collective-permute-start(f32[32,3072]{1,0:T(8,128)S(1)} %collective-permute-done.2.refs_3_), channel_id=1, source_target_pairs={{0,6},{2,0},{4,2},{6,4},{1,7},{3,1},{5,3},{7,5},{8,14},{10,8},{12,... | collective-permute-start | bytes 1179656 | tf_op jit(solution)/shard_map/ppermute | solution.py:386
  29.3 0.7 copy-start.13
  29.3 0.9 copy-start.14
  30.2 0.8 copy-start.15
  38.3 2.9 %copy-start.2 = (f32[32,3072]{1,0:T(8,128)}, f32[32,3072]{1,0:T(8,128)S(1)}, u32[]{:S(2)}) copy-start(f32[32,3072]{1,0:T(8,128)S(1)} %collective-permute-done.1.refs_0_.refs_6_) | copy-start | bytes 1179652
  38.3 2.9 %copy-start.3 = (f32[32,3072]{1,0:T(8,128)}, f32[32,3072]{1,0:T(8,128)S(1)}, u32[]{:S(2)}) copy-start(f32[32,3072]{1,0:T(8,128)S(1)} %collective-permute-done.3.refs_1_.refs_7_) | copy-start | bytes 1179652
  38.3 2.4 %collective-permute-start.11 = (f32[32,3072]{1,0:T(8,128)S(1)}, f32[32,3072]{1,0:T(8,128)S(1)}, u32[]{:S(2)}, u32[]{:S(2)}) collective-permute-start(f32[32,3072]{1,0:T(8,128)S(1)} %collective-permute-done.1.refs_0_.refs_6_), channel_id=1, source_target_pairs={{0,1},{1,0},{2,3},{3,2},{4,5},{5,4},{6,7},{7,6},{8,9},{9,8},{10,11... | collective-permute-start | bytes 1179656 | tf_op jit(solution)/shard_map/ppermute | solution.py:386
  39.3 1.9 %collective-permute-start.12 = (f32[32,3072]{1,0:T(8,128)S(1)}, f32[32,3072]{1,0:T(8,128)S(1)}, u32[]{:S(2)}, u32[]{:S(2)}) collective-permute-start(f32[32,3072]{1,0:T(8,128)S(1)} %collective-permute-done.3.refs_1_.refs_7_), channel_id=1, source_target_pairs={{0,1},{1,0},{2,3},{3,2},{4,5},{5,4},{6,7},{7,6},{8,9},{9,8},{10,11... | collective-permute-start | bytes 1179656 | tf_op jit(solution)/shard_map/ppermute | solution.py:386
  40.7 0.8 copy-start.4
  41.2 0.8 copy-start.5
  79.6 17.9 %all-to-all-start.2 = ((f32[32,32,128]{2,1,0:T(8,128)}), f32[32,32,128]{2,1,0:T(8,128)S(1)}, u32[]{:S(2)}, u32[]{:S(2)}) async-start(f32[32,32,128]{2,1,0:T(8,128)} %get-tuple-element.33), calls=%async_computation.2 | async-start | bytes 1048576 | tf_op jit(solution)/shard_map/all_to_all | solution.py:394
  83.5 5.1 %collective-permute-start.15 = (f32[32,8,128]{2,1,0:T(8,128)S(1)}, f32[32,8,128]{2,1,0:T(8,128)S(1)}, u32[]{:S(2)}, u32[]{:S(2)}) collective-permute-start(f32[32,8,128]{2,1,0:T(8,128)S(1)} %all_to_all.21), channel_id=1, source_target_pairs={{0,2},{2,4},{4,6},{6,0},{1,3},{3,5},{5,7},{7,1},{8,10},{10,12},{12... | collective-permute-start | bytes 393224 | tf_op jit(solution)/shard_map/ppermute | solution.py:386
  84.5 7.0 %collective-permute-start.14 = (f32[32,8,128]{2,1,0:T(8,128)S(1)}, f32[32,8,128]{2,1,0:T(8,128)S(1)}, u32[]{:S(2)}, u32[]{:S(2)}) collective-permute-start(f32[32,8,128]{2,1,0:T(8,128)S(1)} %all_to_all.21), channel_id=1, source_target_pairs={{0,4},{2,6},{4,0},{6,2},{1,5},{3,7},{5,1},{7,3},{8,12},{10,14},{12... | collective-permute-start | bytes 393224 | tf_op jit(solution)/shard_map/ppermute | solution.py:386
  87.5 4.1 %collective-permute-start.13 = (f32[32,8,128]{2,1,0:T(8,128)S(1)}, f32[32,8,128]{2,1,0:T(8,128)S(1)}, u32[]{:S(2)}, u32[]{:S(2)}) collective-permute-start(f32[32,8,128]{2,1,0:T(8,128)S(1)} %all_to_all.21), channel_id=1, source_target_pairs={{0,6},{2,0},{4,2},{6,4},{1,7},{3,1},{5,3},{7,5},{8,14},{10,8},{12,... | collective-permute-start | bytes 393224 | tf_op jit(solution)/shard_map/ppermute | solution.py:386
  91.6 15.4 %copy-start = (f32[4,32,8,128]{3,2,1,0:T(8,128)}, f32[4,32,8,128]{3,2,1,0:T(8,128)S(1)}, u32[]{:S(2)}) copy-start(f32[4,32,8,128]{3,2,1,0:T(8,128)S(1)} %pad_maximum_fusion.mine_ref) | copy-start | bytes 1572868
  91.6 15.4 %collective-permute-start.16 = (f32[4,32,8,128]{3,2,1,0:T(8,128)S(1)}, f32[4,32,8,128]{3,2,1,0:T(8,128)S(1)}, u32[]{:S(2)}, u32[]{:S(2)}) collective-permute-start(f32[4,32,8,128]{3,2,1,0:T(8,128)S(1)} %pad_maximum_fusion.mine_ref), channel_id=1, source_target_pairs={{0,1},{1,0},{2,3},{3,2},{4,5},{5,4},{6,7},{7,6},{8,9},{9,8},{10,11... | collective-permute-start | bytes 1572872 | tf_op jit(solution)/shard_map/ppermute | solution.py:386
  98.4 31.2 %all-to-all-start.3 = ((f32[32,32,128]{2,1,0:T(8,128)}), f32[32,32,128]{2,1,0:T(8,128)S(1)}, u32[]{:S(2)}, u32[]{:S(2)}) async-start(f32[32,32,128]{2,1,0:T(8,128)} %broadcast_in_dim.8), calls=%async_computation.3 | async-start | bytes 1048576 | tf_op jit(solution)/shard_map/all_to_all | solution.py:395
  107.1 0.8 copy-start.7
  129.7 0.8 copy-start.1

commit v4 on v3

--- a/solution.py
+++ b/solution.py
@@ -164,8 +164,7 @@
 
 
 def dot6(left, right):
-    rows = left.shape[0]
-    left, right = thirds(left), thirds(right)
+    rows = left[0].shape[0]
     first = product(jnp.concatenate(left, axis=0), right[0])
     second = product(jnp.concatenate(left[:2], axis=0), right[1])
     small = first[2 * rows :] + (second[rows:] + product(left[0], right[2]))
@@ -335,10 +334,10 @@
             slot = 64 * (2 * dy + other)
             to = pl.multiple_of(column(dy, other), 64)
             hold_ref[pl.ds(to, 64), :] = proj[slot : slot + 64]
-    inverse = inverse_ref[...]
-    coupling = dot6(inverse, hold_ref[...])
+    inverse = thirds(inverse_ref[...])
+    coupling = dot6(inverse, thirds(hold_ref[...]))
     coupling_ref[...] = coupling
-    both_ref[:cols], both_ref[cols:] = halves(dot6(coupling.T, inverse))
+    both_ref[:cols], both_ref[cols:] = halves(dot6(thirds(coupling.T), inverse))
 
     def send(k):
         part = chunk(k, depth)

time: 141 us -> 141 us (level)
  no operation moved by 1% of the time
where the time goes in v4:
time: 141 us
  Pallas kernels  44.3 us (31%)
  starting transfers between devices  37.2 us (26%)
  blocking collectives  31.8 us (23%)
  waiting for transfers between devices  19.8 us (14%)
  local copies, waits for them, and re-layouts  5.98 us (4%)
    ppermute x17, starting transfers between devices, shift(): lax.ppermute(value, axis, [(i, (i + step) % length) for i in range(length)])  24.7 us
    pallas_call x1, Pallas kernels, factor(): pl.pallas_call(factor_kernel, out_shape=[jax.ShapeDtypeStruct((size, size...  21.8 us
    ppermute x17, waiting for transfers between devices, shift(): lax.ppermute(value, axis, [(i, (i + step) % length) for i in range(length)])  18.9 us
    all_to_all x1, blocking collectives, sum_over_rows(): summed = jnp.sum(lax.all_to_all(pieces, ('z', 'x'), 0, 0), axis=0)  18.8 us
    all_to_all x1, blocking collectives, sum_over_rows(): lax.all_to_all(jnp.broadcast_to(summed, pieces.shape), ('z', 'x'), 0, 0)  13 us
    pallas_call x1, Pallas kernels, update(): pl.pallas_call(update_kernel, out_shape=[float_shape(size, cols), float_s...  10.3 us
    all_to_all x1, starting transfers between devices, sum_over_rows(): lax.all_to_all(jnp.broadcast_to(summed, pieces.shape), ('z', 'x'), 0, 0)  8.62 us
    pallas_call x1, Pallas kernels, project_first(): pl.pallas_call(first_kernel, out_shape=[float_shape(*shape) for shape in...  6.54 us
  transfers between devices with their start and end apart: 19, of which 9 were waited for; matrix products, arithmetic and copies ran while one was open for 2% of the time, Pallas kernels for 20%

profile of v4, /device:TPU:1, one launch (start us, length us, event | category | flops | bytes accessed | tf_op | source)
XLA Modules:
  0.0 140.9 jit_solution(5750779227453238270)
XLA Ops:
  0.6 3.3 %collective-permute-start.4 = (f32[64,3072]{1,0:T(8,128)}, f32[64,3072]{1,0:T(8,128)S(1)}, u32[]{:S(2)}, u32[]{:S(2)}) collective-permute-start(f32[64,3072]{1,0:T(8,128)} %bitcast.7), channel_id=1, source_target_pairs={{0,1},{1,0},{2,3},{3,2},{4,5},{5,4},{6,7},{7,6},{8,9},{9,8},{10,11... | collective-permute-start | bytes 2359304 | tf_op jit(solution)/shard_map/ppermute | solution.py:385
  4.0 1.2 fusion
  5.1 0.1 collective-permute-start
  5.2 2.7 %collective-permute-start.2 = (f32[32,3072]{1,0:T(8,128)S(1)}, f32[32,3072]{1,0:T(8,128)S(1)}, u32[]{:S(2)}, u32[]{:S(2)}) collective-permute-start(f32[32,3072]{1,0:T(8,128)S(1)} %get-tuple-element.22), channel_id=1, source_target_pairs={{0,6},{2,0},{4,2},{6,4},{1,7},{3,1},{5,3},{7,5},{8,14},{10,8},{12,... | collective-permute-start | bytes 1179656 | tf_op jit(solution)/shard_map/ppermute | solution.py:385
  7.9 0.0 collective-permute-done.4.refs_1_
  7.9 0.1 collective-permute-start.5
  8.0 1.4 collective-permute-start.8
  9.4 6.7 %collective-permute-done.2.refs_3_ = f32[32,3072]{1,0:T(8,128)S(1)} collective-permute-done((f32[32,3072]{1,0:T(8,128)S(1)}, f32[32,3072]{1,0:T(8,128)S(1)}, u32[]{:S(2)}, u32[]{:S(2)}) %collective-permute-start.2) | collective-permute-done | bytes 393248 | tf_op jit(solution)/shard_map/ppermute | solution.py:385
  16.1 1.8 %collective-permute-start.7 = (f32[32,3072]{1,0:T(8,128)S(1)}, f32[32,3072]{1,0:T(8,128)S(1)}, u32[]{:S(2)}, u32[]{:S(2)}) collective-permute-start(f32[32,3072]{1,0:T(8,128)S(1)} %collective-permute-done.2.refs_3_), channel_id=1, source_target_pairs={{0,1},{1,0},{2,3},{3,2},{4,5},{5,4},{6,7},{7,6},{8,9},{9,8},{10,11... | collective-permute-start | bytes 1179656 | tf_op jit(solution)/shard_map/ppermute | solution.py:385
  17.9 0.0 collective-permute-done.refs_6_.refs_10_
  17.9 0.4 collective-permute-start.9
  18.4 6.2 %collective-permute-done.5.refs_2_ = f32[32,3072]{1,0:T(8,128)S(1)} collective-permute-done((f32[32,3072]{1,0:T(8,128)S(1)}, f32[32,3072]{1,0:T(8,128)S(1)}, u32[]{:S(2)}, u32[]{:S(2)}) %collective-permute-start.5) | collective-permute-done | bytes 393248 | tf_op jit(solution)/shard_map/ppermute | solution.py:385
  24.5 1.1 collective-permute-start.6
  25.6 0.7 collective-permute-start.10
  26.4 2.9 %collective-permute-start.3 = (f32[32,3072]{1,0:T(8,128)S(1)}, f32[32,3072]{1,0:T(8,128)S(1)}, u32[]{:S(2)}, u32[]{:S(2)}) collective-permute-start(f32[32,3072]{1,0:T(8,128)S(1)} %collective-permute-done.2.refs_3_), channel_id=1, source_target_pairs={{0,6},{2,0},{4,2},{6,4},{1,7},{3,1},{5,3},{7,5},{8,14},{10,8},{12,... | collective-permute-start | bytes 1179656 | tf_op jit(solution)/shard_map/ppermute | solution.py:385
  29.3 0.7 copy-done.13
  30.0 0.1 copy-done.14
  30.2 0.8 copy-done.15
  30.9 6.5 %project_first.1 = (f32[384,256]{1,0:T(8,128)}, f32[384,64]{1,0:T(8,128)}) custom-call(f32[3072,256]{1,0:T(8,128)} %trailing_ref.5, f32[64,3072]{1,0:T(8,128)} %bitcast.9, f32[64,3072]{1,0:T(8,128)} %copy-done.6, f32[32,3072]{1,0:T(8,128)} %copy-done.10, f32[32,3072]{1,0:T(8,128)} %copy-done.9, f32[32,3072]{1,0:T(8,128)} %copy-done.14, ...), custom_call_target="tpu_custom_call" | custom-call | flops 15000000512 | bytes 6000000 | tf_op jit(solution)/shard_map/project_first/pallas_call | solution.py:272
  37.5 0.8 collective-permute-done.1.refs_0_.refs_6_
  38.3 1.0 collective-permute-start.11
  39.3 0.1 collective-permute-start.12
  39.4 1.2 collective-permute-done.11.refs_2_.refs_8_
  40.7 0.6 collective-permute-done.12.refs_3_.refs_9_
  41.2 0.2 copy-done.4
  41.4 0.6 copy-done.5
  42.0 5.8 %project_last.1 = (f32[32,32,128]{2,1,0:T(8,128)}, f32[32,8,128]{2,1,0:T(8,128)}) custom-call(s32[1]{0:T(128)} %bitcast.1.core_ref, f32[3072,256]{1,0:T(8,128)} %trailing_ref.5, f32[32,3072]{1,0:T(8,128)} %copy-done.2, f32[32,3072]{1,0:T(8,128)} %copy-done.3, f32[32,3072]{1,0:T(8,128)} %copy-done.4, f32[32,3072]{1,0:T(8,128)} %copy-done.5, ...), custom_call_target="tpu_custom_call" | custom-call | flops 1000000000 | bytes 6000000 | tf_op jit(solution)/shard_map/project_last/pallas_call | solution.py:291
  47.8 18.8 %all_to_all.20 = f32[32,8,128]{2,1,0:T(8,128)S(1)} all-to-all(f32[32,8,128]{2,1,0:T(8,128)} %get-tuple-element.29), channel_id=1, replica_groups=mesh['z'=8,'x'=4,'y'=4,'core'=2] {'z','x'}, dimensions={0} | all-to-all | bytes 262144 | tf_op jit(solution)/shard_map/all_to_all | solution.py:393
  66.6 13.0 %all_to_all.21 = f32[32,8,128]{2,1,0:T(8,128)S(1)} all-to-all(f32[32,8,128]{2,1,0:T(8,128)S(1)} %broadcast_in_dim.7), channel_id=1, replica_groups=mesh['z'=8,'x'=4,'y'=4,'core'=2] {'z','x'}, dimensions={0} | all-to-all | bytes 262144 | tf_op jit(solution)/shard_map/all_to_all | solution.py:394
  79.6 3.9 %all-to-all-start.2 = ((f32[32,32,128]{2,1,0:T(8,128)}), f32[32,32,128]{2,1,0:T(8,128)S(1)}, u32[]{:S(2)}, u32[]{:S(2)}) async-start(f32[32,32,128]{2,1,0:T(8,128)} %get-tuple-element.33), calls=%async_computation.2 | async-start | bytes 1048576 | tf_op jit(solution)/shard_map/all_to_all | solution.py:393
  83.5 1.0 collective-permute-start.15
  84.5 2.9 %collective-permute-start.14 = (f32[32,8,128]{2,1,0:T(8,128)S(1)}, f32[32,8,128]{2,1,0:T(8,128)S(1)}, u32[]{:S(2)}, u32[]{:S(2)}) collective-permute-start(f32[32,8,128]{2,1,0:T(8,128)S(1)} %all_to_all.21), channel_id=1, source_target_pairs={{0,4},{2,6},{4,0},{6,2},{1,5},{3,7},{5,1},{7,3},{8,12},{10,14},{12... | collective-permute-start | bytes 393224 | tf_op jit(solution)/shard_map/ppermute | solution.py:385
  87.5 0.8 collective-permute-start.13
  88.2 0.4 collective-permute-done.15
  88.6 2.9 %collective-permute-done.14 = f32[32,8,128]{2,1,0:T(8,128)S(1)} collective-permute-done((f32[32,8,128]{2,1,0:T(8,128)S(1)}, f32[32,8,128]{2,1,0:T(8,128)S(1)}, u32[]{:S(2)}, u32[]{:S(2)}) %collective-permute-start.14) | collective-permute-done | bytes 131104 | tf_op jit(solution)/shard_map/ppermute | solution.py:385
  91.5 0.1 collective-permute-done.13
  91.6 0.1 pad_maximum_fusion.mine_ref
  91.6 0.0 copy-start
  91.6 4.4 %collective-permute-start.16 = (f32[4,32,8,128]{3,2,1,0:T(8,128)S(1)}, f32[4,32,8,128]{3,2,1,0:T(8,128)S(1)}, u32[]{:S(2)}, u32[]{:S(2)}) collective-permute-start(f32[4,32,8,128]{3,2,1,0:T(8,128)S(1)} %pad_maximum_fusion.mine_ref), channel_id=1, source_target_pairs={{0,1},{1,0},{2,3},{3,2},{4,5},{5,4},{6,7},{7,6},{8,9},{9,8},{10,11... | collective-permute-start | bytes 1572872 | tf_op jit(solution)/shard_map/ppermute | solution.py:385
  96.0 0.6 pad_add_fusion.place_ref
  96.7 0.9 all-to-all-done.2
  97.6 0.9 broadcast_in_dim.8
  98.4 8.6 %all-to-all-start.3 = ((f32[32,32,128]{2,1,0:T(8,128)}), f32[32,32,128]{2,1,0:T(8,128)S(1)}, u32[]{:S(2)}, u32[]{:S(2)}) async-start(f32[32,32,128]{2,1,0:T(8,128)} %broadcast_in_dim.8), calls=%async_computation.3 | async-start | bytes 1048576 | tf_op jit(solution)/shard_map/all_to_all | solution.py:394
  107.1 0.0 copy-start.7
  107.1 0.8 copy-done.7
  107.9 21.8 %factor.1 = (f32[512,512]{1,0:T(8,128)}, f32[512,512]{1,0:T(8,128)}) custom-call(s32[2]{0:T(128)} %pad_add_fusion.place_ref, f32[4,32,8,128]{3,2,1,0:T(8,128)} %copy-done, f32[4,32,8,128]{3,2,1,0:T(8,128)} %copy-done.7), custom_call_target="tpu_custom_call" | custom-call | flops 24999999488 | bytes 4000000 | tf_op jit(solution)/shard_map/factor/pallas_call | solution.py:123
  129.7 0.8 copy-done.1
  130.5 10.3 %update.1 = (f32[512,256]{1,0:T(8,128)}, f32[3072,256]{1,0:T(8,128)}) custom-call(s32[2]{0:T(128)} %pad_add_fusion.place_ref, f32[32,32,128]{2,1,0:T(8,128)} %copy-done.1, f32[512,512]{1,0:T(8,128)} %get-tuple-element.34.inverse_ref, f32[3072,256]{1,0:T(8,128)} %trailing_ref.5, f32[64,3072]{1,0:T(8,128)} %bitcast.11, f32[64,3072]{1,0:T(8,128)} %copy-done.6, ...), custom_call_target="tpu_custom_call" | custom-call | flops 3000000000 | bytes 13000000 | tf_op jit(solution)/shard_map/update/pallas_call | solution.py:360
  (35 shorter events, 0.2 us)
Async XLA Ops:
  0.6 7.3 %collective-permute-start.4 = (f32[64,3072]{1,0:T(8,128)}, f32[64,3072]{1,0:T(8,128)S(1)}, u32[]{:S(2)}, u32[]{:S(2)}) collective-permute-start(f32[64,3072]{1,0:T(8,128)} %bitcast.7), channel_id=1, source_target_pairs={{0,1},{1,0},{2,3},{3,2},{4,5},{5,4},{6,7},{7,6},{8,9},{9,8},{10,11... | collective-permute-start | bytes 2359304 | tf_op jit(solution)/shard_map/ppermute | solution.py:385
  5.1 12.8 %collective-permute-start = (f32[32,3072]{1,0:T(8,128)S(1)}, f32[32,3072]{1,0:T(8,128)S(1)}, u32[]{:S(2)}, u32[]{:S(2)}) collective-permute-start(f32[32,3072]{1,0:T(8,128)S(1)} %get-tuple-element.21), channel_id=1, source_target_pairs={{0,2},{2,4},{4,6},{6,0},{1,3},{3,5},{5,7},{7,1},{8,10},{10,12},{12... | collective-permute-start | bytes 1179656 | tf_op jit(solution)/shard_map/ppermute | solution.py:385
  5.2 10.9 %collective-permute-start.2 = (f32[32,3072]{1,0:T(8,128)S(1)}, f32[32,3072]{1,0:T(8,128)S(1)}, u32[]{:S(2)}, u32[]{:S(2)}) collective-permute-start(f32[32,3072]{1,0:T(8,128)S(1)} %get-tuple-element.22), channel_id=1, source_target_pairs={{0,6},{2,0},{4,2},{6,4},{1,7},{3,1},{5,3},{7,5},{8,14},{10,8},{12,... | collective-permute-start | bytes 1179656 | tf_op jit(solution)/shard_map/ppermute | solution.py:385
  7.9 21.4 %copy-start.6 = (f32[64,3072]{1,0:T(8,128)}, f32[64,3072]{1,0:T(8,128)S(1)}, u32[]{:S(2)}) copy-start(f32[64,3072]{1,0:T(8,128)S(1)} %collective-permute-done.4.refs_1_) | copy-start | bytes 2359300
  7.9 16.6 %collective-permute-start.5 = (f32[32,3072]{1,0:T(8,128)S(1)}, f32[32,3072]{1,0:T(8,128)S(1)}, u32[]{:S(2)}, u32[]{:S(2)}) collective-permute-start(f32[32,3072]{1,0:T(8,128)S(1)} %get-tuple-element.21), channel_id=1, source_target_pairs={{0,6},{2,0},{4,2},{6,4},{1,7},{3,1},{5,3},{7,5},{8,14},{10,8},{12,... | collective-permute-start | bytes 1179656 | tf_op jit(solution)/shard_map/ppermute | solution.py:385
  8.0 17.7 %collective-permute-start.8 = (f32[32,3072]{1,0:T(8,128)S(1)}, f32[32,3072]{1,0:T(8,128)S(1)}, u32[]{:S(2)}, u32[]{:S(2)}) collective-permute-start(f32[32,3072]{1,0:T(8,128)S(1)} %get-tuple-element.22), channel_id=1, source_target_pairs={{0,2},{2,4},{4,6},{6,0},{1,3},{3,5},{5,7},{7,1},{8,10},{10,12},{12... | collective-permute-start | bytes 1179656 | tf_op jit(solution)/shard_map/ppermute | solution.py:385
  16.1 13.2 %copy-start.9 = (f32[32,3072]{1,0:T(8,128)}, f32[32,3072]{1,0:T(8,128)S(1)}, u32[]{:S(2)}) copy-start(f32[32,3072]{1,0:T(8,128)S(1)} %collective-permute-done.2.refs_3_) | copy-start | bytes 1179652
  16.1 10.3 %collective-permute-start.7 = (f32[32,3072]{1,0:T(8,128)S(1)}, f32[32,3072]{1,0:T(8,128)S(1)}, u32[]{:S(2)}, u32[]{:S(2)}) collective-permute-start(f32[32,3072]{1,0:T(8,128)S(1)} %collective-permute-done.2.refs_3_), channel_id=1, source_target_pairs={{0,1},{1,0},{2,3},{3,2},{4,5},{5,4},{6,7},{7,6},{8,9},{9,8},{10,11... | collective-permute-start | bytes 1179656 | tf_op jit(solution)/shard_map/ppermute | solution.py:385
  17.9 11.4 %copy-start.8 = (f32[32,3072]{1,0:T(8,128)}, f32[32,3072]{1,0:T(8,128)S(1)}, u32[]{:S(2)}) copy-start(f32[32,3072]{1,0:T(8,128)S(1)} %collective-permute-done.refs_6_.refs_10_) | copy-start | bytes 1179652
  17.9 11.3 %collective-permute-start.9 = (f32[32,3072]{1,0:T(8,128)S(1)}, f32[32,3072]{1,0:T(8,128)S(1)}, u32[]{:S(2)}, u32[]{:S(2)}) collective-permute-start(f32[32,3072]{1,0:T(8,128)S(1)} %collective-permute-done.refs_6_.refs_10_), channel_id=1, source_target_pairs={{0,1},{1,0},{2,3},{3,2},{4,5},{5,4},{6,7},{7,6},{8,9},{9,8},{10,11... | collective-permute-start | bytes 1179656 | tf_op jit(solution)/shard_map/ppermute | solution.py:385
  24.5 4.8 %copy-start.10 = (f32[32,3072]{1,0:T(8,128)}, f32[32,3072]{1,0:T(8,128)S(1)}, u32[]{:S(2)}) copy-start(f32[32,3072]{1,0:T(8,128)S(1)} %collective-permute-done.5.refs_2_) | copy-start | bytes 1179652
  24.5 4.7 %collective-permute-start.6 = (f32[32,3072]{1,0:T(8,128)S(1)}, f32[32,3072]{1,0:T(8,128)S(1)}, u32[]{:S(2)}, u32[]{:S(2)}) collective-permute-start(f32[32,3072]{1,0:T(8,128)S(1)} %collective-permute-done.5.refs_2_), channel_id=1, source_target_pairs={{0,1},{1,0},{2,3},{3,2},{4,5},{5,4},{6,7},{7,6},{8,9},{9,8},{10,11... | collective-permute-start | bytes 1179656 | tf_op jit(solution)/shard_map/ppermute | solution.py:385
  25.6 3.7 %copy-start.11 = (f32[32,3072]{1,0:T(8,128)}, f32[32,3072]{1,0:T(8,128)S(1)}, u32[]{:S(2)}) copy-start(f32[32,3072]{1,0:T(8,128)S(1)} %collective-permute-done.8.refs_7_.refs_11_) | copy-start | bytes 1179652
  25.6 3.6 %collective-permute-start.10 = (f32[32,3072]{1,0:T(8,128)S(1)}, f32[32,3072]{1,0:T(8,128)S(1)}, u32[]{:S(2)}, u32[]{:S(2)}) collective-permute-start(f32[32,3072]{1,0:T(8,128)S(1)} %collective-permute-done.8.refs_7_.refs_11_), channel_id=1, source_target_pairs={{0,1},{1,0},{2,3},{3,2},{4,5},{5,4},{6,7},{7,6},{8,9},{9,8},{10,11... | collective-permute-start | bytes 1179656 | tf_op jit(solution)/shard_map/ppermute | solution.py:385
  26.4 11.9 %collective-permute-start.1 = (f32[32,3072]{1,0:T(8,128)S(1)}, f32[32,3072]{1,0:T(8,128)S(1)}, u32[]{:S(2)}, u32[]{:S(2)}) collective-permute-start(f32[32,3072]{1,0:T(8,128)S(1)} %collective-permute-done.refs_6_.refs_10_), channel_id=1, source_target_pairs={{0,2},{2,4},{4,6},{6,0},{1,3},{3,5},{5,7},{7,1},{8,10},{10,12},{12... | collective-permute-start | bytes 1179656 | tf_op jit(solution)/shard_map/ppermute | solution.py:385
  26.4 3.0 %copy-start.12 = (f32[32,3072]{1,0:T(8,128)}, f32[32,3072]{1,0:T(8,128)S(1)}, u32[]{:S(2)}) copy-start(f32[32,3072]{1,0:T(8,128)S(1)} %collective-permute-done.7.refs_5_) | copy-start | bytes 1179652
  26.4 11.9 %collective-permute-start.3 = (f32[32,3072]{1,0:T(8,128)S(1)}, f32[32,3072]{1,0:T(8,128)S(1)}, u32[]{:S(2)}, u32[]{:S(2)}) collective-permute-start(f32[32,3072]{1,0:T(8,128)S(1)} %collective-permute-done.2.refs_3_), channel_id=1, source_target_pairs={{0,6},{2,0},{4,2},{6,4},{1,7},{3,1},{5,3},{7,5},{8,14},{10,8},{12,... | collective-permute-start | bytes 1179656 | tf_op jit(solution)/shard_map/ppermute | solution.py:385
  29.3 0.7 copy-start.13
  29.3 0.9 copy-start.14
  30.2 0.8 copy-start.15
  38.3 2.9 %copy-start.2 = (f32[32,3072]{1,0:T(8,128)}, f32[32,3072]{1,0:T(8,128)S(1)}, u32[]{:S(2)}) copy-start(f32[32,3072]{1,0:T(8,128)S(1)} %collective-permute-done.1.refs_0_.refs_6_) | copy-start | bytes 1179652
  38.3 2.9 %copy-start.3 = (f32[32,3072]{1,0:T(8,128)}, f32[32,3072]{1,0:T(8,128)S(1)}, u32[]{:S(2)}) copy-start(f32[32,3072]{1,0:T(8,128)S(1)} %collective-permute-done.3.refs_1_.refs_7_) | copy-start | bytes 1179652
  38.3 2.4 %collective-permute-start.11 = (f32[32,3072]{1,0:T(8,128)S(1)}, f32[32,3072]{1,0:T(8,128)S(1)}, u32[]{:S(2)}, u32[]{:S(2)}) collective-permute-start(f32[32,3072]{1,0:T(8,128)S(1)} %collective-permute-done.1.refs_0_.refs_6_), channel_id=1, source_target_pairs={{0,1},{1,0},{2,3},{3,2},{4,5},{5,4},{6,7},{7,6},{8,9},{9,8},{10,11... | collective-permute-start | bytes 1179656 | tf_op jit(solution)/shard_map/ppermute | solution.py:385
  39.3 1.9 %collective-permute-start.12 = (f32[32,3072]{1,0:T(8,128)S(1)}, f32[32,3072]{1,0:T(8,128)S(1)}, u32[]{:S(2)}, u32[]{:S(2)}) collective-permute-start(f32[32,3072]{1,0:T(8,128)S(1)} %collective-permute-done.3.refs_1_.refs_7_), channel_id=1, source_target_pairs={{0,1},{1,0},{2,3},{3,2},{4,5},{5,4},{6,7},{7,6},{8,9},{9,8},{10,11... | collective-permute-start | bytes 1179656 | tf_op jit(solution)/shard_map/ppermute | solution.py:385
  40.7 0.8 copy-start.4
  41.2 0.8 copy-start.5
  79.6 17.9 %all-to-all-start.2 = ((f32[32,32,128]{2,1,0:T(8,128)}), f32[32,32,128]{2,1,0:T(8,128)S(1)}, u32[]{:S(2)}, u32[]{:S(2)}) async-start(f32[32,32,128]{2,1,0:T(8,128)} %get-tuple-element.33), calls=%async_computation.2 | async-start | bytes 1048576 | tf_op jit(solution)/shard_map/all_to_all | solution.py:393
  83.5 5.1 %collective-permute-start.15 = (f32[32,8,128]{2,1,0:T(8,128)S(1)}, f32[32,8,128]{2,1,0:T(8,128)S(1)}, u32[]{:S(2)}, u32[]{:S(2)}) collective-permute-start(f32[32,8,128]{2,1,0:T(8,128)S(1)} %all_to_all.21), channel_id=1, source_target_pairs={{0,2},{2,4},{4,6},{6,0},{1,3},{3,5},{5,7},{7,1},{8,10},{10,12},{12... | collective-permute-start | bytes 393224 | tf_op jit(solution)/shard_map/ppermute | solution.py:385
  84.5 7.0 %collective-permute-start.14 = (f32[32,8,128]{2,1,0:T(8,128)S(1)}, f32[32,8,128]{2,1,0:T(8,128)S(1)}, u32[]{:S(2)}, u32[]{:S(2)}) collective-permute-start(f32[32,8,128]{2,1,0:T(8,128)S(1)} %all_to_all.21), channel_id=1, source_target_pairs={{0,4},{2,6},{4,0},{6,2},{1,5},{3,7},{5,1},{7,3},{8,12},{10,14},{12... | collective-permute-start | bytes 393224 | tf_op jit(solution)/shard_map/ppermute | solution.py:385
  87.5 4.1 %collective-permute-start.13 = (f32[32,8,128]{2,1,0:T(8,128)S(1)}, f32[32,8,128]{2,1,0:T(8,128)S(1)}, u32[]{:S(2)}, u32[]{:S(2)}) collective-permute-start(f32[32,8,128]{2,1,0:T(8,128)S(1)} %all_to_all.21), channel_id=1, source_target_pairs={{0,6},{2,0},{4,2},{6,4},{1,7},{3,1},{5,3},{7,5},{8,14},{10,8},{12,... | collective-permute-start | bytes 393224 | tf_op jit(solution)/shard_map/ppermute | solution.py:385
  91.6 15.4 %copy-start = (f32[4,32,8,128]{3,2,1,0:T(8,128)}, f32[4,32,8,128]{3,2,1,0:T(8,128)S(1)}, u32[]{:S(2)}) copy-start(f32[4,32,8,128]{3,2,1,0:T(8,128)S(1)} %pad_maximum_fusion.mine_ref) | copy-start | bytes 1572868
  91.6 15.4 %collective-permute-start.16 = (f32[4,32,8,128]{3,2,1,0:T(8,128)S(1)}, f32[4,32,8,128]{3,2,1,0:T(8,128)S(1)}, u32[]{:S(2)}, u32[]{:S(2)}) collective-permute-start(f32[4,32,8,128]{3,2,1,0:T(8,128)S(1)} %pad_maximum_fusion.mine_ref), channel_id=1, source_target_pairs={{0,1},{1,0},{2,3},{3,2},{4,5},{5,4},{6,7},{7,6},{8,9},{9,8},{10,11... | collective-permute-start | bytes 1572872 | tf_op jit(solution)/shard_map/ppermute | solution.py:385
  98.4 31.2 %all-to-all-start.3 = ((f32[32,32,128]{2,1,0:T(8,128)}), f32[32,32,128]{2,1,0:T(8,128)S(1)}, u32[]{:S(2)}, u32[]{:S(2)}) async-start(f32[32,32,128]{2,1,0:T(8,128)} %broadcast_in_dim.8), calls=%async_computation.3 | async-start | bytes 1048576 | tf_op jit(solution)/shard_map/all_to_all | solution.py:394
  107.1 0.8 copy-start.7
  129.7 0.8 copy-start.1
